TPU v7x, 128 devices: a whole 4x4x4 slice. The times are simulated.
128 devices in a mesh: region: 16 (over y, z_hi, core), gx: 4 (over x), gy: 2 (over z_lo).
Axes of the slice: x: 4, y: 4, z: 4 (z_hi: 2, z_lo: 2; z = z_hi * 2 + z_lo), core: 2. Of those that a mesh axis runs over, the one named last changes fastest.
Arguments:
- cap_source: float32 [64, 2048, 1024], P('region', 'gx', 'gy'), may hold values from 0.02 to 2
- cap_sink: float32 [64, 2048, 1024], P('region', 'gx', 'gy'), may hold values from 0.02 to 2
- penalty: float32 [64, 2048, 1024], P('region', 'gx', 'gy'), may hold values from 0.2 to 2
- labels: float32 [64, 2048, 1024], P('region', 'gx', 'gy'), may hold values from 0 to 1
- multiplier: float32 [16, 2048, 1024], P('region', 'gx', 'gy'), may hold values from -3 to 3
Outputs:
- labels_out: float32 [64, 2048, 1024], P('region', 'gx', 'gy')
- multiplier_out: float32 [16, 2048, 1024], P('region', 'gx', 'gy')
All inputs are finite; a program needn't handle non-finite values.
Results may differ from a plain program's by a relative error of at most 0.00002.
Values sent between devices are 32-bit elements; how exact they have to be, the bound alone decides.
A program may use at most 256 MiB of HBM per device.

v0:
```python
import functools

import jax
import jax.numpy as jnp
from jax import lax
from jax.experimental import pallas as pl
from jax.experimental.pallas import tpu as pltpu
from jax.sharding import PartitionSpec as P

MESH = pl.DeviceIdType.MESH
ITERS = 3
CC = 0.3
STEP = 0.16
RHO = 0.5
EPSILON = 1e-06

LANES = 128
TOP = 16
HALO = 8
SLOT = 6
SPAN = 32
GROUPS = 11
WIDE = 176
BLOCK = 128
CHUNKS = 4


def lane_of(rows):
    return lax.broadcasted_iota(jnp.int32, (rows, LANES), 1)


def kernel(
    sizes,
    cap_source,
    cap_sink,
    penalty,
    labels,
    multiplier,
    out,
    mult,
    lab,
    src,
    snk,
    pen,
    px,
    py,
    pz,
    jj,
    pt,
    own_lam,
    low_lam,
    above,
    pack,
    other,
    wl,
    wp,
    ws,
    wk,
    ww,
    wt,
    wpx,
    wpz,
    wj,
    wpy,
    packed,
    packed_low,
    part,
    got_a,
    got_b,
    load_sem,
    lam_load_sem,
    halo_send,
    halo_recv,
    lam_send,
    lam_recv,
    win_send,
    win_recv,
    fwd_send,
    fwd_recv,
    up_send,
    up_recv,
    red_send_a,
    red_recv_a,
    red_send_b,
    red_recv_b,
):
    n_region, n_x, n_y = sizes
    depth, width_x, width_y = labels.shape
    tiles = width_y // LANES
    end = TOP + width_x
    first_row = TOP - HALO
    steps = (width_x + 2 * HALO) // WIDE
    r, x, y = lax.axis_index("region"), lax.axis_index("gx"), lax.axis_index("gy")
    up, down = lax.rem(r + 1, n_region), lax.rem(r + n_region - 1, n_region)
    x_next, x_prev = lax.rem(x + 1, n_x), lax.rem(x + n_x - 1, n_x)
    y_other = 1 - y
    group_a = [(dx, dy) for dx in range(n_x) for dy in range(n_y) if dx or dy]
    peers_a = [(r, lax.rem(x + dx, n_x), lax.rem(y + dy, n_y)) for dx, dy in group_a]
    peers_b = [(lax.rem(r + d, n_region), x, y) for d in range(1, n_region)]

    barrier = pltpu.get_barrier_semaphore()
    for peer in peers_a + peers_b:
        pl.semaphore_signal(barrier, inc=1, device_id=peer, device_id_type=MESH)
    pl.semaphore_wait(barrier, len(peers_a) + len(peers_b))

    def remote(a, b, s, t, device):
        return pltpu.make_async_remote_copy(a, b, s, t, device_id=device, device_id_type=MESH)

    edge_tile = (1 - y) * (tiles - 1)
    arrays = ((labels, lab), (penalty, pen), (cap_source, src), (cap_sink, snk))
    loads = []
    own_copy = pltpu.make_async_copy(multiplier.at[0], own_lam.at[TOP:end], lam_load_sem)
    for i in range(tiles):
        t = lax.rem(edge_tile + i, tiles)
        column = pl.ds(pl.multiple_of(t * LANES, LANES), LANES)
        for q, (whole, held) in enumerate(arrays):
            copy = pltpu.make_async_copy(whole.at[:, :, column], held.at[:, t, TOP:end, :], load_sem.at[q, i])
            copy.start()
            loads.append(copy)
        if i == 0:
            own_copy.start()

    rows_of = width_x // CHUNKS
    lam_copies = []
    for c in range(CHUNKS):
        copy = remote(
            multiplier.at[0, c * rows_of : (c + 1) * rows_of],
            low_lam.at[TOP + c * rows_of : TOP + (c + 1) * rows_of],
            lam_send.at[c],
            lam_recv.at[c],
            (up, x, y),
        )
        copy.start()
        lam_copies.append(copy)

    halo_waits = []
    for side, (device, take, put) in enumerate(
        (
            ((r, x_prev, y), slice(0, HALO), slice(end, end + HALO)),
            ((r, x_next, y), slice(width_x - HALO, width_x), slice(TOP - HALO, TOP)),
        )
    ):
        copy = remote(multiplier.at[0, take], own_lam.at[put], halo_send.at[4, side, 0], halo_recv.at[4, side, 0], device)
        copy.start()
        halo_waits.append(copy)
        for q, (whole, held) in enumerate(arrays):
            for t in range(tiles):
                copy = remote(
                    whole.at[:, take, t * LANES : (t + 1) * LANES],
                    held.at[:, t, put, :],
                    halo_send.at[q, side, t],
                    halo_recv.at[q, side, t],
                    device,
                )
                copy.start()
                halo_waits.append(copy)

    for copy in loads[: len(arrays)]:
        copy.wait()
    own_copy.wait()

    def pack_rows(i, carry):
        row = pl.multiple_of(TOP + i * BLOCK, 8)
        lane = lane_of(BLOCK)
        value = None
        for z in range(depth):
            for q, (_, held) in enumerate(arrays):
                at = SPAN * z + SLOT * q
                moved = pltpu.roll(held[z, edge_tile, pl.ds(row, BLOCK), :], (at + 3) % LANES, 1)
                value = moved if value is None else jnp.where(lane >= at, moved, value)
        at = SPAN * (depth - 1) + SLOT * len(arrays)
        column = pl.ds(pl.multiple_of(edge_tile * LANES, LANES), LANES)
        moved = pltpu.roll(own_lam[pl.ds(row, BLOCK), column], (at + 3) % LANES, 1)
        value = jnp.where(lane >= at, moved, value)
        pack[pl.ds(row, BLOCK), :] = value
        return carry

    lax.fori_loop(0, width_x // BLOCK, pack_rows, 0)
    window = []
    for n, (take, target, put, device) in enumerate(
        (
            (slice(TOP, end), other, slice(TOP, end), (r, x, y_other)),
            (slice(TOP, TOP + HALO), other, slice(end, end + HALO), (r, x_prev, y_other)),
            (slice(end - HALO, end), other, slice(TOP - HALO, TOP), (r, x_next, y_other)),
            (slice(TOP, TOP + HALO), pack, slice(end, end + HALO), (r, x_prev, y)),
            (slice(end - HALO, end), pack, slice(TOP - HALO, TOP), (r, x_next, y)),
        )
    ):
        copy = remote(pack.at[take], target.at[put], win_send.at[n], win_recv.at[n], device)
        copy.start()
        window.append(copy)

    for copy in loads[len(arrays) :]:
        copy.wait()
    for copy in halo_waits:
        copy.wait()
    forwards = []
    for n, put in enumerate((slice(TOP - HALO, TOP), slice(end, end + HALO))):
        copy = remote(own_lam.at[put], low_lam.at[put], fwd_send.at[n], fwd_recv.at[n], (up, x, y))
        copy.start()
        forwards.append(copy)
    for copy in window:
        copy.wait()

    has_above = (r < n_region - 1).astype(jnp.float32)
    has_below = (r > 0).astype(jnp.float32)
    not_first_x = (x > 0).astype(jnp.float32)
    is_last_x = x == n_x - 1
    not_first_y = (y > 0).astype(jnp.float32)
    is_last_y = y == n_y - 1
    lam_lane = SPAN * (depth - 1)

    def make_window(i, carry):
        row = pl.multiple_of(first_row + i * WIDE, 8)
        rows = pl.ds(row, WIDE)
        lane = lane_of(WIDE)
        rest = lane & (SPAN - 1)
        j = rest - SLOT * ((rest * 43) >> 8)
        mine = (j < 3) == (y == 0)
        both = jnp.where(mine, pack[rows, :], other[rows, :])
        wl[rows, :] = both
        wp[rows, :] = pltpu.roll(both, LANES - SLOT, 1)
        ws[rows, :] = pltpu.roll(both, LANES - 2 * SLOT, 1)
        lam = pltpu.roll(both, LANES - 4 * SLOT, 1)
        lam = jnp.where((lane >= lam_lane) & (lane < lam_lane + SLOT), lam * has_above, 0.0)
        wk[rows, :] = pltpu.roll(both, LANES - 3 * SLOT, 1) + lam
        small = lane_of(8)
        for d in range(WIDE // (8 * GROUPS)):
            value = None
            for g in range(GROUPS):
                n = 8 * (d * GROUPS + g)
                moved = pltpu.roll(both[n : n + 8], (8 * g - (lam_lane + 4 * SLOT)) % LANES, 1)
                value = moved if value is None else jnp.where(small >= 8 * g, moved, value)
            at = pl.multiple_of(i * (WIDE // GROUPS) + 8 * d, 8)
            packed[pl.ds(at, 8), :] = value
        return carry

    lax.fori_loop(0, steps, make_window, 0)
    copy = remote(packed, packed_low, fwd_send.at[2], fwd_recv.at[2], (up, x, y))
    copy.start()
    forwards.append(copy)

    def hold_last(ref, *at):
        here = ref[(*at, pl.ds(end, 8), slice(None))]
        last = ref[(*at, pl.ds(end - 1, 8), slice(None))]
        ref[(*at, pl.ds(end, 8), slice(None))] = jnp.where(is_last_x, last, here)

    for z in range(depth):
        for t in range(tiles):
            hold_last(lab, z, t)
    hold_last(wl)

    scale = STEP / CC

    def ascend(k, z, row, count):
        rows, after = pl.ds(row, count), pl.ds(row + 1, count)
        lane = lane_of(count)
        field = jj if k else lab
        side = wj.at[k - 1] if k else wl
        here = [field[z, t, rows, :] for t in range(tiles)]
        rolled = [pltpu.roll(v, LANES - 1, 1) for v in here]
        rolled.append(pltpu.roll(side[rows, :], LANES - 1 - (SPAN * z + 3), 1))
        for t in range(tiles):
            j = here[t]
            jx = field[z, t, after, :]
            jy = jnp.where(lane == LANES - 1, rolled[t + 1], rolled[t])
            if k:
                qx = px[z, t, rows, :] + (jx - j)
                dy = jy - j
            else:
                qx = (j - jx) * scale
                dy = (j - jy) * scale
            if t == tiles - 1:
                dy = jnp.where((lane == LANES - 1) & is_last_y, 0.0, dy)
            qy = py[z, t, rows, :] + dy if k else dy
            square = qx * qx + qy * qy
            if z < depth - 1:
                jz = field[z + 1, t, rows, :]
                qz = pz[z, t, rows, :] + (jz - j) if k else (j - jz) * scale
                square = square + qz * qz
            factor = jnp.minimum(pen[z, t, rows, :] * lax.rsqrt(square), 1.0)
            px[z, t, rows, :] = qx * factor
            py[z, t, rows, :] = qy * factor
            if z < depth - 1:
                pz[z, t, rows, :] = qz * factor

    def ascend_all(k, z):
        def step(i, carry):
            ascend(k, z, pl.multiple_of(first_row + i * WIDE, 8), WIDE)
            return carry

        lax.fori_loop(0, steps, step, 0)
        for t in range(tiles):
            px[z, t, first_row:TOP, :] = px[z, t, first_row:TOP, :] * not_first_x

    def descend(k, z, row, count, total):
        rows, before = pl.ds(row, count), pl.ds(row - 1, count)
        lane = lane_of(count)
        here = [py[z, t, rows, :] for t in range(tiles)]
        rolled = [pltpu.roll(v, 1, 1) for v in here]
        rolled.insert(0, pltpu.roll(wpy[k, rows, :], LANES - (SPAN * z + 2), 1) * not_first_y)
        for t in range(tiles):
            columns = slice(t * LANES, (t + 1) * LANES)
            dv = px[z, t, rows, :] - px[z, t, before, :] + (here[t] - jnp.where(lane == 0, rolled[t], rolled[t + 1]))
            if z < depth - 1:
                dv = dv + pz[z, t, rows, :]
            if z > 0:
                dv = dv - pz[z - 1, t, rows, :]
            source, sink = src[z, t, rows, :], snk[z, t, rows, :]
            if k:
                w, flow = lab[z, t, rows, :], pt[z, t, rows, :]
            else:
                if z == 0:
                    sink = sink - low_lam[rows, columns] * has_below
                if z == depth - 1:
                    sink = sink + own_lam[rows, columns] * has_above
                if z in (0, depth - 1):
                    snk[z, t, rows, :] = sink
                w, flow = lab[z, t, rows, :] * (1.0 / CC), jnp.minimum(source, sink)
            level = jnp.minimum(source - dv + w, flow + 1.0 / CC)
            after = jnp.maximum(level - sink, 0.0)
            if k < ITERS - 1:
                pt[z, t, rows, :] = jnp.minimum(sink, level)
                lab[z, t, rows, :] = after
                jj[z, t, rows, :] = w * STEP - after * (2.0 * STEP)
            else:
                out[z, pl.ds(row - TOP, count), columns] = after * CC
                total = total + jnp.abs(w - after)
        return total

    def descend_all(k, z):
        def step(i, carry):
            descend(k, z, pl.multiple_of(first_row + i * WIDE, 8), WIDE, None)
            return carry

        lax.fori_loop(0, steps, step, 0)
        for t in range(tiles):
            hold_last(jj, z, t)

    def descend_last(z, total):
        def step(i, carry):
            return descend(ITERS - 1, z, pl.multiple_of(TOP + i * BLOCK, 8), BLOCK, carry)

        return lax.fori_loop(0, width_x // BLOCK, step, total)

    side_rows = slice(first_row, end + HALO)
    side_after = slice(first_row + 1, end + HALO + 1)
    side_before = slice(first_row - 1, end + HALO - 1)
    side_lane = lane_of(end + HALO - first_row)

    def ascend_side(k):
        field = wj.at[k - 1] if k else wl
        j = field[side_rows, :]
        jx = field[side_after, :]
        jy = pltpu.roll(j, LANES - 1, 1)
        jz = pltpu.roll(j, LANES - SPAN, 1)
        if k:
            qx = wpx[side_rows, :] + (jx - j)
            qy = wpy[k - 1, side_rows, :] + (jy - j)
            qz = wpz[side_rows, :] + (jz - j)
        else:
            qx, qy, qz = (j - jx) * scale, (j - jy) * scale, (j - jz) * scale
        qz = jnp.where(side_lane < lam_lane, qz, 0.0)
        factor = jnp.minimum(wp[side_rows, :] * lax.rsqrt(qx * qx + qy * qy + qz * qz), 1.0)
        wpx[side_rows, :] = qx * factor
        wpy[k, side_rows, :] = qy * factor
        wpz[side_rows, :] = qz * factor
        wpx[first_row:TOP, :] = wpx[first_row:TOP, :] * not_first_x

    def descend_side(k):
        qy, qz = wpy[k, side_rows, :], wpz[side_rows, :]
        dv = wpx[side_rows, :] - wpx[side_before, :] + (qy - pltpu.roll(qy, 1, 1)) + (qz - pltpu.roll(qz, SPAN, 1))
        source, sink = ws[side_rows, :], wk[side_rows, :]
        if k:
            w, flow = ww[side_rows, :], wt[side_rows, :]
        else:
            w, flow = wl[side_rows, :] * (1.0 / CC), jnp.minimum(source, sink)
        level = jnp.minimum(source - dv + w, flow + 1.0 / CC)
        after = jnp.maximum(level - sink, 0.0)
        wt[side_rows, :] = jnp.minimum(sink, level)
        ww[side_rows, :] = after
        wj[k, side_rows, :] = w * STEP - after * (2.0 * STEP)
        hold_last(wj, k)

    for z in range(depth):
        ascend_all(0, z)
    ascend_side(0)
    for z in range(1, depth):
        descend_all(0, z)

    for copy in forwards:
        copy.wait()
    small = lane_of(8)
    for n in range((width_x + 2 * HALO) // 8):
        d, g = n // GROUPS, n % GROUPS
        lam = pltpu.roll(packed_low[8 * d : 8 * d + 8, :], (LANES - 8 * g) % LANES, 1)
        rows = slice(first_row + 8 * n, first_row + 8 * n + 8)
        wk[rows, :] = wk[rows, :] - jnp.where(small < SLOT, lam * has_below, 0.0)
    descend_side(0)
    ascend_side(1)
    descend_side(1)
    ascend_side(2)

    ascend_all(1, 1)
    for copy in lam_copies:
        copy.wait()
    total = jnp.zeros((BLOCK, LANES), jnp.float32)
    descend_all(0, 0)
    ascend_all(1, 0)
    descend_all(1, 0)
    descend_all_late = functools.partial(descend_all, 1)
    descend_all_late(1)
    ascend_all(2, 0)
    total = descend_last(0, total)
    copy_up = remote(out.at[0], above, up_send, up_recv, (down, x, y))
    copy_up.start()
    ascend_all(1, 2)
    ascend_all(1, 3)
    descend_all(1, 2)
    descend_all(1, 3)
    for z in range(1, depth):
        ascend_all(2, z)
    for z in range(1, depth):
        total = descend_last(z, total)
    copy_up.wait()

    def gap_of(i, carry):
        rows = pl.ds(pl.multiple_of(i * BLOCK, 8), BLOCK)
        gap = (out[depth - 1, rows, :] - above[rows, :]) * has_above
        above[rows, :] = gap
        squares = gap * gap
        for t in range(tiles):
            carry = carry + squares[:, t * LANES : (t + 1) * LANES]
        return carry

    gaps = lax.fori_loop(0, width_x // BLOCK, gap_of, jnp.zeros((BLOCK, LANES), jnp.float32))
    gap_row = jnp.sum(gaps, axis=0, keepdims=True)
    err_row = jnp.sum(total, axis=0, keepdims=True)
    sub = lax.broadcasted_iota(jnp.int32, (8, LANES), 0)
    mine = jnp.where(sub == 0, gap_row, jnp.where(sub == 1, err_row, 0.0))

    for peers, got, send, recv in ((peers_a, got_a, red_send_a, red_recv_a), (peers_b, got_b, red_send_b, red_recv_b)):
        here = part.at[0 if got is got_a else 1]
        here[...] = mine
        copies = []
        for n, peer in enumerate(peers):
            copy = remote(here, got.at[n], send.at[n], recv.at[n], peer)
            copy.start()
            copies.append(copy)
        for copy in copies:
            copy.wait()
        for n in range(len(peers)):
            mine = mine + got[n]

    sums = jnp.sum(mine, axis=1, keepdims=True)
    all_cells = depth * width_x * width_y * n_region * n_x * n_y
    plane_cells = (n_region - 1) * width_x * n_x * width_y * n_y
    err = sums[1:2, :] * (CC / all_cells)
    msq = sums[0:1, :] * (1.0 / plane_cells)
    rate = RHO * err * lax.rsqrt(msq + EPSILON)

    def write(i, carry):
        rows = pl.ds(pl.multiple_of(i * BLOCK, 8), BLOCK)
        lam_rows = pl.ds(pl.multiple_of(TOP + i * BLOCK, 8), BLOCK)
        mult[0, rows, :] = own_lam[lam_rows, :] * has_above + above[rows, :] * rate
        return carry

    lax.fori_loop(0, width_x // BLOCK, write, 0)


def on_device(sizes, cap_source, cap_sink, penalty, labels, multiplier):
    depth, width_x, width_y = labels.shape
    tiles = width_y // LANES
    rows = TOP + width_x + TOP
    n_region, n_x, n_y = sizes

    def vmem(*shape):
        return pltpu.VMEM(shape, jnp.float32)

    def dma(*shape):
        return pltpu.SemaphoreType.DMA(shape) if shape else pltpu.SemaphoreType.DMA

    volume = vmem(depth, tiles, rows, LANES)
    plane = vmem(rows, width_y)
    strip = vmem(rows, LANES)
    peers_a, peers_b = n_x * n_y - 1, n_region - 1
    compact = vmem((width_x + 2 * HALO) // GROUPS, LANES)
    return pl.pallas_call(
        functools.partial(kernel, sizes),
        out_shape=[
            jax.ShapeDtypeStruct(labels.shape, jnp.float32),
            jax.ShapeDtypeStruct(multiplier.shape, jnp.float32),
        ],
        in_specs=[pl.BlockSpec(memory_space=pl.ANY)] * 5,
        out_specs=[pl.BlockSpec(memory_space=pltpu.VMEM)] * 2,
        scratch_shapes=[
            volume,
            volume,
            volume,
            volume,
            volume,
            volume,
            vmem(depth - 1, tiles, rows, LANES),
            volume,
            volume,
            plane,
            plane,
            vmem(width_x, width_y),
            strip,
            strip,
            strip,
            strip,
            strip,
            strip,
            strip,
            strip,
            strip,
            strip,
            vmem(2, rows, LANES),
            vmem(3, rows, LANES),
            compact,
            compact,
            vmem(2, 8, LANES),
            vmem(peers_a, 8, LANES),
            vmem(peers_b, 8, LANES),
            dma(4, tiles),
            dma(),
            dma(5, 2, tiles),
            dma(5, 2, tiles),
            dma(CHUNKS),
            dma(CHUNKS),
            dma(5),
            dma(5),
            dma(3),
            dma(3),
            dma(),
            dma(),
            dma(peers_a),
            dma(peers_a),
            dma(peers_b),
            dma(peers_b),
        ],
        compiler_params=pltpu.CompilerParams(collective_id=0, has_side_effects=True, vmem_limit_bytes=60 << 20),
        name="slab_flow",
    )(cap_source, cap_sink, penalty, labels, multiplier)


def solution(mesh):
    placed = P("region", "gx", "gy")
    sizes = tuple(mesh.shape[a] for a in ("region", "gx", "gy"))
    return jax.shard_map(
        functools.partial(on_device, sizes),
        mesh=mesh,
        in_specs=(placed,) * 5,
        out_specs=(placed, placed),
        check_vma=False,
    )
```

profile of v0, /device:TPU:0, one launch (start us, length us, event | category | flops | bytes accessed | tf_op | source)
XLA Modules:
  0.0 73.5 jit_solution(17647868664689269995)
XLA Ops:
  0.6 67.2 %slab_flow.1 = (f32[4,512,512]{2,1,0:T(8,128)}, f32[1,512,512]{2,1,0:T(8,128)}) custom-call(f32[4,512,512]{2,1,0:T(8,128)} %cap_source.1, f32[4,512,512]{2,1,0:T(8,128)} %cap_sink.1, f32[4,512,512]{2,1,0:T(8,128)} %penalty.1, f32[4,512,512]{2,1,0:T(8,128)} %labels.1, f32[1,512,512]{2,1,0:T(8,128)} %multiplier.1), custom_call_target="tpu_custom_call" | custom-call | tf_op jit(solution)/shard_map/slab_flow/pallas_call | solution.py:488
  67.8 0.0 copy-start
  67.8 4.7 %copy.9 = f32[4,512,512]{2,1,0:T(8,128)} copy(f32[4,512,512]{2,1,0:T(8,128)} %get-tuple-element.4) | data formatting | bytes 8388608
  72.5 0.0 copy-done
  72.5 1.0 %copy.10 = f32[1,512,512]{2,1,0:T(8,128)} copy(f32[1,512,512]{2,1,0:T(8,128)S(1)} %copy-done) | data formatting | bytes 2097152
Async XLA Ops:
  67.8 4.7 %copy-start = (f32[1,512,512]{2,1,0:T(8,128)S(1)}, f32[1,512,512]{2,1,0:T(8,128)}, u32[]{:S(2)}) copy-start(f32[1,512,512]{2,1,0:T(8,128)} %get-tuple-element.5) | copy-start | bytes 3145732
where the time goes:
time: 74.6 us; the launch traced here: 73.5 us
  Pallas kernels  67.2 us (90%)
  local copies, waits for them, and re-layouts  5.7 us (8%)
    pallas_call x1, Pallas kernels, on_device(): pl.pallas_call(functools.partial(kernel, sizes), out_shape=[jax.ShapeDtyp...  67.2 us
    unnamed x4, local copies, waits for them, and re-layouts  5.7 us

commit v1 on v0

v1 whole, which is shorter than its diff:
```python
import functools

import jax
import jax.numpy as jnp
from jax import lax
from jax.experimental import pallas as pl
from jax.experimental.pallas import tpu as pltpu
from jax.sharding import PartitionSpec as P

MESH = pl.DeviceIdType.MESH
ITERS = 3
CC = 0.3
STEP = 0.16
RHO = 0.5
EPSILON = 1e-06

LANES = 128
TOP = 32
BOTTOM = 24
HALO = 8
SLOT = 6
SPAN = 32
GROUPS = 11
WIDE = 176
BLOCK = 128
CHUNKS = 4
CHUNK = 136
EARLY = 4


def lane_of(rows):
    return lax.broadcasted_iota(jnp.int32, (rows, LANES), 1)


def kernel(
    sizes,
    cap_source,
    cap_sink,
    penalty,
    labels,
    multiplier,
    out,
    mult,
    lab,
    src,
    snk,
    pen,
    px,
    py,
    pz,
    jj,
    pt,
    own_lam,
    low_lam,
    above,
    halo,
    pack,
    sent,
    other,
    wl,
    wp,
    ws,
    wk,
    ww,
    wt,
    wpx,
    wpz,
    wj,
    wpy,
    packed,
    packed_low,
    part,
    got,
    load_sem,
    lam_load_sem,
    halo_send,
    halo_recv,
    lam_send,
    lam_recv,
    win_send,
    win_recv,
    fwd_send,
    fwd_recv,
    up_send,
    up_recv,
    red_send,
    red_recv,
):
    n_region, n_x, n_y = sizes
    depth, width_x, width_y = labels.shape
    tiles = width_y // LANES
    end = TOP + width_x
    first_row = TOP - HALO
    wide_rows = width_x + 2 * HALO
    steps = wide_rows // WIDE
    r, x, y = lax.axis_index("region"), lax.axis_index("gx"), lax.axis_index("gy")
    up, down = lax.rem(r + 1, n_region), lax.rem(r + n_region - 1, n_region)
    x_next, x_prev = lax.rem(x + 1, n_x), lax.rem(x + n_x - 1, n_x)
    y_other = 1 - y
    core, high, high_y = lax.rem(r, 2), lax.rem(r // 2, 2), r // 4
    n_rows = n_region // 4
    stages = (
        [(4 * high_y + 2 * high + (1 - core), x, y)],
        [(r, lax.rem(x + d, n_x), y) for d in range(1, n_x)],
        [(4 * lax.rem(high_y + d, n_rows) + 2 * high + core, x, y) for d in range(1, n_rows)],
        [
            (r, x, y_other),
            (4 * high_y + 2 * (1 - high) + core, x, y),
            (4 * high_y + 2 * (1 - high) + core, x, y_other),
        ],
    )

    barrier = pltpu.get_barrier_semaphore()
    friends = [(up, x, y), (down, x, y), (up, x, y_other), (down, x, y_other)]
    friends += [peer for stage in stages[1:] for peer in stage]
    for peer in friends:
        pl.semaphore_signal(barrier, inc=1, device_id=peer, device_id_type=MESH)

    def remote(a, b, s, t, device):
        return pltpu.make_async_remote_copy(a, b, s, t, device_id=device, device_id_type=MESH)

    edge_tile = (1 - y) * (tiles - 1)
    arrays = ((labels, lab), (penalty, pen), (cap_source, src), (cap_sink, snk))
    loads = []

    def load(i):
        t = lax.rem(edge_tile + i, tiles)
        column = pl.ds(pl.multiple_of(t * LANES, LANES), LANES)
        for q, (whole, held) in enumerate(arrays):
            copy = pltpu.make_async_copy(whole.at[:, :, column], held.at[:, t, TOP:end, :], load_sem.at[q, i])
            copy.start()
            loads.append(copy)

    own_copy = pltpu.make_async_copy(multiplier.at[0], own_lam.at[TOP:end], lam_load_sem)
    own_copy.start()
    load(0)
    pl.semaphore_wait(barrier, len(friends))

    lam_halo, edge_halo, rest_halo = [], [], []
    sides = (
        ((r, x_prev, y), slice(0, HALO), slice(end, end + HALO)),
        ((r, x_next, y), slice(width_x - HALO, width_x), slice(TOP - HALO, TOP)),
    )
    for side, (device, take, put) in enumerate(sides):
        copy = remote(multiplier.at[0, take], own_lam.at[put], halo_send.at[4, side, 0], halo_recv.at[4, side, 0], device)
        copy.start()
        lam_halo.append(copy)
    lam_bounds = [0] + [CHUNK * c - HALO for c in range(1, CHUNKS)] + [width_x]
    lam_copies = [
        remote(multiplier.at[0, a:b], low_lam.at[TOP + a : TOP + b], lam_send.at[c], lam_recv.at[c], (up, x, y))
        for c, (a, b) in enumerate(zip(lam_bounds[:-1], lam_bounds[1:]))
    ]
    for copy in lam_copies[:EARLY]:
        copy.start()
    edge_column = pl.ds(pl.multiple_of(edge_tile * LANES, LANES), LANES)
    rest_column = pl.ds(pl.multiple_of(y * LANES, LANES), (tiles - 1) * LANES)
    for column, which, copies in ((edge_column, 0, edge_halo), (rest_column, 1, rest_halo)):
        for side, (device, take, put) in enumerate(sides):
            for q, (whole, _) in enumerate(arrays):
                copy = remote(
                    whole.at[:, take, column],
                    halo.at[q, side, :, :, column],
                    halo_send.at[q, side, which],
                    halo_recv.at[q, side, which],
                    device,
                )
                copy.start()
                copies.append(copy)
    for i in range(1, tiles):
        load(i)

    def place_halo(t, column):
        for side, (_, _, put) in enumerate(sides):
            for q, (_, held) in enumerate(arrays):
                for z in range(depth):
                    held[z, t, put, :] = halo[q, side, z, :, column]

    own_copy.wait()
    for copy in lam_halo:
        copy.wait()
    forwards = []
    for n, put in enumerate((slice(TOP - HALO, TOP), slice(end, end + HALO))):
        copy = remote(own_lam.at[put], low_lam.at[put], fwd_send.at[n], fwd_recv.at[n], (up, x, y))
        copy.start()
        forwards.append(copy)
    small = lane_of(8)
    for d in range(wide_rows // (8 * GROUPS)):
        value = None
        for g in range(GROUPS):
            row = first_row + 8 * (d * GROUPS + g)
            moved = pltpu.roll(own_lam[row : row + 8, edge_column], (8 * g + 3) % LANES, 1)
            value = moved if value is None else jnp.where(small >= 8 * g, moved, value)
        packed[8 * d : 8 * d + 8, :] = value
    for n, device in enumerate(((up, x, y), (up, x, y_other))):
        copy = remote(packed, packed_low.at[n], fwd_send.at[2 + n], fwd_recv.at[2 + n], device)
        copy.start()
        forwards.append(copy)

    for copy in loads[: len(arrays)]:
        copy.wait()
    for copy in edge_halo:
        copy.wait()
    place_halo(edge_tile, edge_column)

    def pack_rows(i, carry):
        row = pl.multiple_of(first_row + i * WIDE, 8)
        lane = lane_of(WIDE)
        value = None
        for z in range(depth):
            for q, (_, held) in enumerate(arrays):
                at = SPAN * z + SLOT * q
                moved = pltpu.roll(held[z, edge_tile, pl.ds(row, WIDE), :], (at + 3) % LANES, 1)
                value = moved if value is None else jnp.where(lane >= at, moved, value)
        at = SPAN * (depth - 1) + SLOT * len(arrays)
        moved = pltpu.roll(own_lam[pl.ds(row, WIDE), edge_column], (at + 3) % LANES, 1)
        pack[pl.ds(row, WIDE), :] = jnp.where(lane >= at, moved, value)
        return carry

    lax.fori_loop(0, steps, pack_rows, 0)

    def mine_of(rows):
        rest = lane_of(rows) & (SPAN - 1)
        j = rest - SLOT * ((rest * 43) >> 8)
        return (j < 3) == (y == 0)

    half = wide_rows // 2
    turn = jnp.where(y == 0, 3, LANES - 3)
    lower = pltpu.roll(pack[first_row + half : end + HALO, :], turn, 1)
    sent[...] = jnp.where(mine_of(half), pack[first_row : first_row + half, :], lower)
    window = remote(sent, other, win_send, win_recv, (r, x, y_other))
    window.start()
    for copy in lam_copies[EARLY:]:
        copy.start()

    has_above = (r < n_region - 1).astype(jnp.float32)
    has_below = (r > 0).astype(jnp.float32)
    not_first_x = (x > 0).astype(jnp.float32)
    is_last_x = x == n_x - 1
    not_first_y = (y > 0).astype(jnp.float32)
    is_last_y = y == n_y - 1
    lam_lane = SPAN * (depth - 1)

    for copy in loads[len(arrays) :]:
        copy.wait()
    for copy in rest_halo:
        copy.wait()
    for i in range(1, tiles):
        t = lax.rem(edge_tile + i, tiles)
        place_halo(t, pl.ds(pl.multiple_of(t * LANES, LANES), LANES))

    def hold_last(ref, *at):
        here = ref[(*at, pl.ds(end, 8), slice(None))]
        last = ref[(*at, pl.ds(end - 1, 8), slice(None))]
        ref[(*at, pl.ds(end, 8), slice(None))] = jnp.where(is_last_x, last, here)

    for z in range(depth):
        for t in range(tiles):
            hold_last(lab, z, t)

    window.wait()
    mine = mine_of(half)
    for n in range(2):
        rows = slice(first_row + n * half, first_row + (n + 1) * half)
        theirs = other[...]
        if n:
            theirs = pltpu.roll(theirs, turn, 1)
        both = jnp.where(mine, pack[rows, :], theirs)
        lane = lane_of(half)
        wl[rows, :] = both
        wp[rows, :] = pltpu.roll(both, LANES - SLOT, 1)
        ws[rows, :] = pltpu.roll(both, LANES - 2 * SLOT, 1)
        lam = pltpu.roll(both, LANES - 4 * SLOT, 1)
        lam = jnp.where((lane >= lam_lane) & (lane < lam_lane + SLOT), lam * has_above, 0.0)
        wk[rows, :] = pltpu.roll(both, LANES - 3 * SLOT, 1) + lam
    hold_last(wl)

    scale = STEP / CC

    def ascend(k, z, row, count):
        rows, after = pl.ds(row, count), pl.ds(row + 1, count)
        lane = lane_of(count)
        if k is None:
            field, side = lab, wl
        else:
            field, side = jj, wj.at[k]
        here = [field[z, t, rows, :] for t in range(tiles)]
        rolled = [pltpu.roll(v, LANES - 1, 1) for v in here]
        rolled.append(pltpu.roll(side[rows, :], LANES - 1 - 3 - SPAN * z, 1))
        top = isinstance(z, int) and z == depth - 1
        for t in range(tiles):
            j = here[t]
            jx = field[z, t, after, :]
            jy = jnp.where(lane == LANES - 1, rolled[t + 1], rolled[t])
            dx, dy = (jx - j, jy - j) if k is not None else ((j - jx) * scale, (j - jy) * scale)
            if t == tiles - 1:
                dy = jnp.where((lane == LANES - 1) & is_last_y, 0.0, dy)
            qx, qy = (px[z, t, rows, :] + dx, py[z, t, rows, :] + dy) if k is not None else (dx, dy)
            square = qx * qx + qy * qy
            if not top:
                jz = field[z + 1 if isinstance(z, int) else jnp.minimum(z + 1, depth - 1), t, rows, :]
                qz = pz[z, t, rows, :] + (jz - j) if k is not None else (j - jz) * scale
                square = square + qz * qz
            factor = jnp.minimum(pen[z, t, rows, :] * lax.rsqrt(square), 1.0)
            px[z, t, rows, :] = qx * factor
            py[z, t, rows, :] = qy * factor
            pz[z, t, rows, :] = jnp.zeros_like(square) if top else qz * factor

    def open_x(z):
        for t in range(tiles):
            px[z, t, first_row:TOP, :] = px[z, t, first_row:TOP, :] * not_first_x

    def close_x(z):
        for t in range(tiles):
            hold_last(jj, z, t)

    def descend(k, z, row, count, total=None, check=False):
        rows, before = pl.ds(row, count), pl.ds(row - 1, count)
        lane = lane_of(count)
        here = [py[z, t, rows, :] for t in range(tiles)]
        rolled = [pltpu.roll(v, 1, 1) for v in here]
        rolled.insert(0, pltpu.roll(wpy[k, rows, :], LANES - 2 - SPAN * z, 1) * not_first_y)
        bottom = isinstance(z, int) and z == 0
        top = isinstance(z, int) and z == depth - 1
        if check:
            index = row + lax.broadcasted_iota(jnp.int32, (count, LANES), 0)
            inside = (index >= TOP) & (index < end)
        for t in range(tiles):
            columns = slice(t * LANES, (t + 1) * LANES)
            dv = px[z, t, rows, :] - px[z, t, before, :] + (here[t] - jnp.where(lane == 0, rolled[t], rolled[t + 1]))
            if not top:
                dv = dv + pz[z, t, rows, :]
            if not bottom:
                dv = dv - pz[z - 1, t, rows, :]
            source, sink = src[z, t, rows, :], snk[z, t, rows, :]
            if k:
                w, flow = lab[z, t, rows, :], pt[z, t, rows, :]
            else:
                if bottom:
                    sink = sink - low_lam[rows, columns] * has_below
                if top:
                    sink = sink + own_lam[rows, columns] * has_above
                if bottom or top:
                    snk[z, t, rows, :] = sink
                w, flow = lab[z, t, rows, :] * (1.0 / CC), jnp.minimum(source, sink)
            level = jnp.minimum(source - dv + w, flow + 1.0 / CC)
            after = jnp.maximum(level - sink, 0.0)
            if k < ITERS - 1:
                pt[z, t, rows, :] = jnp.minimum(sink, level)
                lab[z, t, rows, :] = after
                jj[z, t, rows, :] = w * STEP - after * (2.0 * STEP)
            else:
                out[z, rows, columns] = after * CC
                change = jnp.abs(w - after)
                total = total + (jnp.where(inside, change, 0.0) if check else change)
        return total

    def planes(low, high, body, finish):
        def plane(z, carry):
            def step(i, inner):
                body(z, pl.multiple_of(first_row + i * WIDE, 8))
                return inner

            lax.fori_loop(0, steps, step, 0)
            finish(z)
            return carry

        if high - low == 1:
            plane(low, 0)
        else:
            lax.fori_loop(low, high, plane, 0)

    def ascend_planes(k, low, high):
        planes(low, high, lambda z, row: ascend(None if k == 0 else k - 1, z, row, WIDE), open_x)

    def descend_planes(k, low, high):
        planes(low, high, lambda z, row: descend(k, z, row, WIDE), close_x)

    def side_step(body):
        def step(i, carry):
            body(pl.multiple_of(first_row + i * WIDE, 8))
            return carry

        lax.fori_loop(0, steps, step, 0)

    side_lane = lane_of(WIDE)

    def ascend_side(k):
        field = wj.at[k - 1] if k else wl

        def body(row):
            rows, after = pl.ds(row, WIDE), pl.ds(row + 1, WIDE)
            j = field[rows, :]
            jx = field[after, :]
            jy = pltpu.roll(j, LANES - 1, 1)
            jz = pltpu.roll(j, LANES - SPAN, 1)
            if k:
                qx = wpx[rows, :] + (jx - j)
                qy = wpy[k - 1, rows, :] + (jy - j)
                qz = wpz[rows, :] + (jz - j)
            else:
                qx, qy, qz = (j - jx) * scale, (j - jy) * scale, (j - jz) * scale
            qz = jnp.where(side_lane < lam_lane, qz, 0.0)
            factor = jnp.minimum(wp[rows, :] * lax.rsqrt(qx * qx + qy * qy + qz * qz), 1.0)
            wpx[rows, :] = qx * factor
            wpy[k, rows, :] = qy * factor
            wpz[rows, :] = qz * factor

        side_step(body)
        wpx[first_row:TOP, :] = wpx[first_row:TOP, :] * not_first_x

    def descend_side(k):
        def body(row):
            rows, before = pl.ds(row, WIDE), pl.ds(row - 1, WIDE)
            qy, qz = wpy[k, rows, :], wpz[rows, :]
            dv = wpx[rows, :] - wpx[before, :] + (qy - pltpu.roll(qy, 1, 1)) + (qz - pltpu.roll(qz, SPAN, 1))
            source, sink = ws[rows, :], wk[rows, :]
            if k:
                w, flow = ww[rows, :], wt[rows, :]
            else:
                w, flow = wl[rows, :] * (1.0 / CC), jnp.minimum(source, sink)
            level = jnp.minimum(source - dv + w, flow + 1.0 / CC)
            after = jnp.maximum(level - sink, 0.0)
            wt[rows, :] = jnp.minimum(sink, level)
            ww[rows, :] = after
            wj[k, rows, :] = w * STEP - after * (2.0 * STEP)

        side_step(body)
        hold_last(wj, k)

    ascend_planes(0, 0, depth - 1)
    ascend_side(0)
    descend_planes(0, 1, depth - 1)
    for copy in forwards:
        copy.wait()
    low_first = jnp.where(y == 0, 0, 1)
    for n in range(wide_rows // 8):
        d, g = n // GROUPS, n % GROUPS
        rows = slice(first_row + 8 * n, first_row + 8 * n + 8)
        merged = jnp.where(
            small < 8 * g + 3, packed_low[low_first, 8 * d : 8 * d + 8, :], packed_low[1 - low_first, 8 * d : 8 * d + 8, :]
        )
        lam = pltpu.roll(merged, (LANES - 8 * g) % LANES, 1)
        wk[rows, :] = wk[rows, :] - jnp.where(small < SLOT, lam * has_below, 0.0)
    descend_side(0)
    ascend_side(1)
    descend_side(1)
    ascend_side(2)
    ascend_planes(1, 1, 2)

    above_bounds = [0] + [CHUNK * c - 3 * HALO for c in range(1, CHUNKS)] + [width_x]
    above_copies = [
        remote(out.at[0, TOP + a : TOP + b], above.at[a:b], up_send.at[c], up_recv.at[c], (down, x, y))
        for c, (a, b) in enumerate(zip(above_bounds[:-1], above_bounds[1:]))
    ]

    def chunk(c, total):
        for n in range(CHUNKS):

            @pl.when(c == n)
            def _():
                lam_copies[n].wait()

        row = pl.multiple_of(first_row + c * CHUNK, 8)
        descend(0, 0, row, CHUNK)
        close_x(0)
        ascend(0, 0, row - 8, CHUNK)
        open_x(0)
        descend(1, 0, row - 8, CHUNK)
        descend(1, 1, row - 8, CHUNK)
        close_x(0)
        close_x(1)
        ascend(1, 0, row - 16, CHUNK)
        open_x(0)
        total = descend(2, 0, row - 16, CHUNK, total, True)
        for n in range(CHUNKS):

            @pl.when(c == n)
            def _():
                above_copies[n].start()

        return total

    total = lax.fori_loop(0, CHUNKS, chunk, jnp.zeros((CHUNK, LANES), jnp.float32))
    err_row = jnp.sum(total, axis=0, keepdims=True)

    ascend_planes(0, depth - 1, depth)
    descend_planes(0, depth - 1, depth)
    ascend_planes(1, 2, depth)
    descend_planes(1, 2, depth)
    ascend_planes(2, 1, depth)

    def last_plane(z, carry):
        def step(i, inner):
            return descend(ITERS - 1, z, pl.multiple_of(TOP + i * BLOCK, 8), BLOCK, inner)

        return lax.fori_loop(0, width_x // BLOCK, step, carry)

    total = lax.fori_loop(1, depth, last_plane, jnp.zeros((BLOCK, LANES), jnp.float32))
    err_row = err_row + jnp.sum(total, axis=0, keepdims=True)
    for copy in above_copies:
        copy.wait()

    def gap_of(i, carry):
        rows = pl.ds(pl.multiple_of(i * BLOCK, 8), BLOCK)
        gap = (out[depth - 1, pl.ds(pl.multiple_of(TOP + i * BLOCK, 8), BLOCK), :] - above[rows, :]) * has_above
        above[rows, :] = gap
        squares = gap * gap
        for t in range(tiles):
            carry = carry + squares[:, t * LANES : (t + 1) * LANES]
        return carry

    gaps = lax.fori_loop(0, width_x // BLOCK, gap_of, jnp.zeros((BLOCK, LANES), jnp.float32))
    gap_row = jnp.sum(gaps, axis=0, keepdims=True)
    sub = lax.broadcasted_iota(jnp.int32, (8, LANES), 0)
    mine = jnp.where(sub == 0, gap_row, jnp.where(sub == 1, err_row, 0.0))
    n = 0
    for s, stage in enumerate(stages):
        part[s] = mine
        copies = []
        for peer in stage:
            copy = remote(part.at[s], got.at[n], red_send.at[n], red_recv.at[n], peer)
            copy.start()
            copies.append((copy, n))
            n += 1
        for copy, slot in copies:
            copy.wait()
        for copy, slot in copies:
            mine = mine + got[slot]

    sums = jnp.sum(mine, axis=1, keepdims=True)
    all_cells = depth * width_x * width_y * n_region * n_x * n_y
    plane_cells = (n_region - 1) * width_x * n_x * width_y * n_y
    err = sums[1:2, :] * (CC / all_cells)
    msq = sums[0:1, :] * (1.0 / plane_cells)
    rate = RHO * err * lax.rsqrt(msq + EPSILON)

    def write(i, carry):
        rows = pl.ds(pl.multiple_of(i * BLOCK, 8), BLOCK)
        lam_rows = pl.ds(pl.multiple_of(TOP + i * BLOCK, 8), BLOCK)
        mult[0, rows, :] = own_lam[lam_rows, :] * has_above + above[rows, :] * rate
        return carry

    lax.fori_loop(0, width_x // BLOCK, write, 0)


def write_out(held, held_mult, out, mult, sem):
    depth, width_x, _ = out.shape
    copies = [pltpu.make_async_copy(held.at[z, TOP : TOP + width_x], out.at[z], sem.at[z]) for z in range(depth)]
    copies.append(pltpu.make_async_copy(held_mult, mult, sem.at[depth]))
    for copy in copies:
        copy.start()
    for copy in copies:
        copy.wait()


def on_device(sizes, cap_source, cap_sink, penalty, labels, multiplier):
    depth, width_x, width_y = labels.shape
    tiles = width_y // LANES
    rows = TOP + width_x + BOTTOM
    n_region, n_x, n_y = sizes

    def vmem(*shape):
        return pltpu.VMEM(shape, jnp.float32)

    def dma(*shape):
        return pltpu.SemaphoreType.DMA(shape) if shape else pltpu.SemaphoreType.DMA

    volume = vmem(depth, tiles, rows, LANES)
    plane = vmem(rows, width_y)
    strip = vmem(rows, LANES)
    half = vmem(width_x // 2 + HALO, LANES)
    peers = 1 + (n_x - 1) + (n_region // 4 - 1) + 3
    compact = (width_x + 2 * HALO) // GROUPS
    held, held_mult = pl.pallas_call(
        functools.partial(kernel, sizes),
        out_shape=[
            pltpu.VMEM((depth, rows, width_y), jnp.float32),
            pltpu.VMEM(multiplier.shape, jnp.float32),
        ],
        in_specs=[pl.BlockSpec(memory_space=pl.ANY)] * 5,
        out_specs=[pl.BlockSpec(memory_space=pltpu.VMEM)] * 2,
        scratch_shapes=[
            volume,
            volume,
            volume,
            volume,
            volume,
            volume,
            volume,
            volume,
            volume,
            plane,
            plane,
            vmem(width_x, width_y),
            vmem(4, 2, depth, HALO, width_y),
            strip,
            half,
            half,
            strip,
            strip,
            strip,
            strip,
            strip,
            strip,
            strip,
            strip,
            vmem(2, rows, LANES),
            vmem(3, rows, LANES),
            vmem(compact, LANES),
            vmem(2, compact, LANES),
            vmem(4, 8, LANES),
            vmem(peers, 8, LANES),
            dma(4, tiles),
            dma(),
            dma(5, 2, 2),
            dma(5, 2, 2),
            dma(CHUNKS),
            dma(CHUNKS),
            dma(),
            dma(),
            dma(4),
            dma(4),
            dma(CHUNKS),
            dma(CHUNKS),
            dma(peers),
            dma(peers),
        ],
        compiler_params=pltpu.CompilerParams(collective_id=0, has_side_effects=True, vmem_limit_bytes=52 << 20),
        name="slab_flow",
    )(cap_source, cap_sink, penalty, labels, multiplier)
    return pl.pallas_call(
        write_out,
        out_shape=[
            jax.ShapeDtypeStruct(labels.shape, jnp.float32),
            jax.ShapeDtypeStruct(multiplier.shape, jnp.float32),
        ],
        in_specs=[pl.BlockSpec(memory_space=pl.ANY)] * 2,
        out_specs=[pl.BlockSpec(memory_space=pl.ANY)] * 2,
        scratch_shapes=[dma(depth + 1)],
        compiler_params=pltpu.CompilerParams(vmem_limit_bytes=4 << 20),
        name="write_out",
    )(held, held_mult)


def solution(mesh):
    placed = P("region", "gx", "gy")
    sizes = tuple(mesh.shape[a] for a in ("region", "gx", "gy"))
    return jax.shard_map(
        functools.partial(on_device, sizes),
        mesh=mesh,
        in_specs=(placed,) * 5,
        out_specs=(placed, placed),
        check_vma=False,
    )
```

time: 74.6 us -> 65.4 us (0.88); the launches traced: 73.5 us -> 65.3 us
  local copies, waits for them, and re-layouts: 5.7 us -> 0 us
  Pallas kernels: 67.2 us -> 64.7 us
    unnamed x4 -> x0, local copies, waits for them, and re-layouts: 5.7 us -> none
    pallas_call x1 -> x2, Pallas kernels: 67.2 us -> 64.7 us  [the longest x1 62.3 us: on_device(): pl.pallas_call(functools.partial(kernel, sizes), out_shape=[pltpu.VMEM((d...]
where the time goes in v1:
time: 65.4 us; the launch traced here: 65.3 us
  Pallas kernels  64.7 us (99%)
    pallas_call x1, Pallas kernels, on_device(): pl.pallas_call(functools.partial(kernel, sizes), out_shape=[pltpu.VMEM((d...  62.3 us
    pallas_call x1, Pallas kernels, on_device(): pl.pallas_call(write_out, out_shape=[jax.ShapeDtypeStruct(labels.shape, j...  2.4 us

profile of v1, /device:TPU:0, one launch (start us, length us, event | category | flops | bytes accessed | tf_op | source)
XLA Modules:
  0.0 65.3 jit_solution(6760904132486139408)
XLA Ops:
  0.6 62.3 %slab_flow.1 = (f32[4,568,512]{2,1,0:T(8,128)S(1)}, f32[1,512,512]{2,1,0:T(8,128)S(1)}) custom-call(f32[4,512,512]{2,1,0:T(8,128)} %cap_source.1, f32[4,512,512]{2,1,0:T(8,128)} %cap_sink.1, f32[4,512,512]{2,1,0:T(8,128)} %penalty.1, f32[4,512,512]{2,1,0:T(8,128)} %labels.1, f32[1,512,512]{2,1,0:T(8,128)} %multiplier.1), custom_call_target="tpu_custom_call" | custom-call | tf_op jit(solution)/shard_map/slab_flow/pallas_call | solution.py:574
  62.9 2.4 %write_out.1 = (f32[4,512,512]{2,1,0:T(8,128)}, f32[1,512,512]{2,1,0:T(8,128)}) custom-call(f32[4,568,512]{2,1,0:T(8,128)S(1)} %get-tuple-element.4.held, f32[1,512,512]{2,1,0:T(8,128)S(1)} %get-tuple-element.5.held_mult), custom_call_target="tpu_custom_call" | custom-call | tf_op jit(solution)/shard_map/write_out/pallas_call | solution.py:631

commit v2 on v1

v2 whole, which is shorter than its diff:
```python
import functools

import jax
import jax.numpy as jnp
from jax import lax
from jax.experimental import pallas as pl
from jax.experimental.pallas import tpu as pltpu
from jax.sharding import PartitionSpec as P

MESH = pl.DeviceIdType.MESH
ITERS = 3
CC = 0.3
STEP = 0.16
RHO = 0.5
EPSILON = 1e-06

LANES = 128
TOP = 32
BOTTOM = 24
HALO = 8
TAKE = 4
SPAN = 32
PART = 10
GROUPS = 11
WIDE = 176
BLOCK = 128
CHUNKS = 4
CHUNK = 136


def lane_of(rows):
    return lax.broadcasted_iota(jnp.int32, (rows, LANES), 1)


def kernel(
    sizes,
    cap_source,
    cap_sink,
    penalty,
    labels,
    multiplier,
    out,
    mult,
    lab,
    src,
    snk,
    pen,
    px,
    py,
    pz,
    jj,
    pt,
    own_lam,
    low_lam,
    above,
    halo,
    sent,
    other,
    wl,
    wp,
    ws,
    wk,
    ww,
    wt,
    wpx,
    wpz,
    wj,
    wpy,
    wu,
    packed,
    packed_low,
    packed_u,
    packed_above,
    part,
    got,
    load_sem,
    lam_load_sem,
    halo_send,
    halo_recv,
    lam_send,
    lam_recv,
    win_send,
    win_recv,
    fwd_send,
    fwd_recv,
    up_send,
    up_recv,
    red_send,
    red_recv,
):
    n_region, n_x, n_y = sizes
    depth, width_x, width_y = labels.shape
    tiles = width_y // LANES
    end = TOP + width_x
    first_row = TOP - HALO
    wide_rows = width_x + 2 * HALO
    steps = wide_rows // WIDE
    r, x, y = lax.axis_index("region"), lax.axis_index("gx"), lax.axis_index("gy")
    up, down = lax.rem(r + 1, n_region), lax.rem(r + n_region - 1, n_region)
    x_next, x_prev = lax.rem(x + 1, n_x), lax.rem(x + n_x - 1, n_x)
    y_other = 1 - y
    core, high, high_y = lax.rem(r, 2), lax.rem(r // 2, 2), r // 4
    n_rows = n_region // 4
    stages = (
        [(4 * high_y + 2 * high + (1 - core), x, y)],
        [(r, lax.rem(x + d, n_x), y) for d in range(1, n_x)],
        [(4 * lax.rem(high_y + d, n_rows) + 2 * high + core, x, y) for d in range(1, n_rows)],
        [
            (r, x, y_other),
            (4 * high_y + 2 * (1 - high) + core, x, y),
            (4 * high_y + 2 * (1 - high) + core, x, y_other),
        ],
    )

    barrier = pltpu.get_barrier_semaphore()
    friends = [(up, x, y), (down, x, y), (up, x, y_other), (down, x, y_other)]
    friends += [peer for stage in stages[1:] for peer in stage]
    for peer in friends:
        pl.semaphore_signal(barrier, inc=1, device_id=peer, device_id_type=MESH)

    def remote(a, b, s, t, device):
        return pltpu.make_async_remote_copy(a, b, s, t, device_id=device, device_id_type=MESH)

    arrays = ((labels, lab), (penalty, pen), (cap_source, src), (cap_sink, snk))
    loads = []

    def load(q):
        whole, held = arrays[q]
        for t in range(tiles):
            column = slice(t * LANES, (t + 1) * LANES)
            copy = pltpu.make_async_copy(whole.at[:, :, column], held.at[:, t, TOP:end, :], load_sem.at[q, t])
            copy.start()
            loads.append(copy)

    load(0)
    load(1)
    pl.semaphore_wait(barrier, len(friends))

    lam_bounds = [0] + [CHUNK * c - HALO for c in range(1, CHUNKS)] + [width_x]
    lam_copies = [
        remote(multiplier.at[0, a:b], low_lam.at[TOP + a : TOP + b], lam_send.at[c], lam_recv.at[c], (up, x, y))
        for c, (a, b) in enumerate(zip(lam_bounds[:-1], lam_bounds[1:]))
    ]
    for copy in lam_copies:
        copy.start()

    sides = (
        ((r, x_prev, y), slice(0, TAKE), slice(0, TAKE), slice(end, end + HALO), slice(end, end + TAKE)),
        ((r, x_next, y), slice(width_x - TAKE, width_x), slice(HALO - TAKE, HALO), slice(TOP - HALO, TOP), slice(TOP - TAKE, TOP)),
    )
    halos = []

    def send_halo(q):
        for side, (device, take, put, _, _) in enumerate(sides):
            copy = remote(arrays[q][0].at[:, take, :], halo.at[q, side, :, put, :], halo_send.at[q, side], halo_recv.at[q, side], device)
            copy.start()
            halos.append(copy)

    def place_halo(q):
        for copy in halos[2 * q : 2 * q + 2]:
            copy.wait()
        for side, (_, _, _, put, _) in enumerate(sides):
            for z in range(depth):
                for t in range(tiles):
                    arrays[q][1][z, t, put, :] = halo[q, side, z, :, t * LANES : (t + 1) * LANES]

    def take_in(q):
        for copy in loads[q * tiles : (q + 1) * tiles]:
            copy.wait()
        place_halo(q)

    send_halo(0)
    send_halo(1)
    load(2)
    load(3)
    own_copy = pltpu.make_async_copy(multiplier.at[0], own_lam.at[TOP:end], lam_load_sem)
    own_copy.start()
    send_halo(2)
    send_halo(3)
    lam_halo = []
    for side, (device, take, _, _, put) in enumerate(sides):
        copy = remote(multiplier.at[0, take], own_lam.at[put], halo_send.at[4, side], halo_recv.at[4, side], device)
        copy.start()
        lam_halo.append(copy)

    has_above = (r < n_region - 1).astype(jnp.float32)
    has_below = (r > 0).astype(jnp.float32)
    not_first_x = (x > 0).astype(jnp.float32)
    is_last_x = x == n_x - 1
    lam_lane = SPAN * (depth - 1)
    edge_tile = (1 - y) * (tiles - 1)
    edge_column = pl.ds(pl.multiple_of(edge_tile * LANES, LANES), LANES)
    small = lane_of(8)

    def turned(value, shift):
        return pltpu.roll(value, lax.rem(shift + 4 * LANES, LANES), 1)

    def hold_last(ref, *at):
        here = ref[(*at, pl.ds(end, 8), slice(None))]
        last = ref[(*at, pl.ds(end - 1, 8), slice(None))]
        ref[(*at, pl.ds(end, 8), slice(None))] = jnp.where(is_last_x, last, here)

    scale = STEP / CC

    def ascend(k, z, row, count):
        rows, after = pl.ds(row, count), pl.ds(row + 1, count)
        lane = lane_of(count)
        field = lab if k == 0 else jj
        here = [field[z, t, rows, :] for t in range(tiles)]
        rolled = [pltpu.roll(v, LANES - 1, 1) for v in here]
        for t in range(tiles):
            j = here[t]
            jx = field[z, t, after, :]
            jy = jnp.where(lane == LANES - 1, rolled[t + 1] if t < tiles - 1 else j, rolled[t])
            dx, dy = (jx - j, jy - j) if k else ((j - jx) * scale, (j - jy) * scale)
            qx, qy = (px[z, t, rows, :] + dx, py[z, t, rows, :] + dy) if k else (dx, dy)
            square = qx * qx + qy * qy
            jz = field[jnp.minimum(z + 1, depth - 1), t, rows, :]
            qz = pz[z, t, rows, :] + (jz - j) if k else (j - jz) * scale
            square = square + qz * qz
            factor = jnp.minimum(pen[z, t, rows, :] * lax.rsqrt(square), 1.0)
            px[z, t, rows, :] = qx * factor
            py[z, t, rows, :] = qy * factor
            pz[z, t, rows, :] = qz * factor

    def open_x(z):
        for t in range(tiles):
            px[z, t, first_row:TOP, :] = px[z, t, first_row:TOP, :] * not_first_x

    def close_x(z):
        for t in range(tiles):
            hold_last(jj, z, t)

    def descend(k, z, row, count, total=None, check=False):
        rows, before = pl.ds(row, count), pl.ds(row - 1, count)
        lane = lane_of(count)
        here = [py[z, t, rows, :] for t in range(tiles)]
        rolled = [pltpu.roll(v, 1, 1) for v in here]
        bottom = isinstance(z, int) and z == 0
        top = isinstance(z, int) and z == depth - 1
        if check:
            index = row + lax.broadcasted_iota(jnp.int32, (count, LANES), 0)
            inside = (index >= TOP) & (index < end)
        for t in range(tiles):
            columns = slice(t * LANES, (t + 1) * LANES)
            dv = px[z, t, rows, :] - px[z, t, before, :] + (here[t] - jnp.where(lane == 0, rolled[t - 1] if t else 0.0, rolled[t]))
            if not top:
                dv = dv + pz[z, t, rows, :]
            if not bottom:
                dv = dv - pz[z - 1, t, rows, :]
            source, sink = src[z, t, rows, :], snk[z, t, rows, :]
            if k:
                w, flow = lab[z, t, rows, :], pt[z, t, rows, :]
            else:
                if bottom:
                    sink = sink - low_lam[rows, columns] * has_below
                if top:
                    sink = sink + own_lam[rows, columns] * has_above
                if bottom or top:
                    snk[z, t, rows, :] = sink
                w, flow = lab[z, t, rows, :] * (1.0 / CC), jnp.minimum(source, sink)
            level = jnp.minimum(source - dv + w, flow + 1.0 / CC)
            after = jnp.maximum(level - sink, 0.0)
            if k < ITERS - 1:
                pt[z, t, rows, :] = jnp.minimum(sink, level)
                lab[z, t, rows, :] = after
                jj[z, t, rows, :] = w * STEP - after * (2.0 * STEP)
            else:
                out[z, rows, columns] = after * CC
                change = jnp.abs(w - after)
                if t == 0:
                    change = jnp.where((lane < 3) & (y == 1), 0.0, change)
                if t == tiles - 1:
                    change = jnp.where((lane >= LANES - 3) & (y == 0), 0.0, change)
                total = total + (jnp.where(inside, change, 0.0) if check else change)
        return total

    def planes(low, high, body, finish):
        def plane(z, carry):
            def step(i, inner):
                body(z, pl.multiple_of(first_row + i * WIDE, 8))
                return inner

            lax.fori_loop(0, steps, step, 0)
            finish(z)
            return carry

        if high - low == 1:
            plane(low, 0)
        else:
            lax.fori_loop(low, high, plane, 0)

    def ascend_planes(k, low, high):
        planes(low, high, lambda z, row: ascend(k, z, row, WIDE), open_x)

    def descend_planes(k, low, high):
        planes(low, high, lambda z, row: descend(k, z, row, WIDE), close_x)

    def side_step(body):
        def step(i, carry):
            body(pl.multiple_of(first_row + i * WIDE, 8))
            return carry

        lax.fori_loop(0, steps, step, 0)

    side_lane = lane_of(WIDE)

    def ascend_side(k):
        field = wj.at[k - 1] if k else wl

        def body(row):
            rows, after = pl.ds(row, WIDE), pl.ds(row + 1, WIDE)
            j = field[rows, :]
            jx = field[after, :]
            jy = pltpu.roll(j, LANES - 1, 1)
            jz = pltpu.roll(j, LANES - SPAN, 1)
            if k:
                qx = wpx[rows, :] + (jx - j)
                qy = wpy[k - 1, rows, :] + (jy - j)
                qz = wpz[rows, :] + (jz - j)
            else:
                qx, qy, qz = (j - jx) * scale, (j - jy) * scale, (j - jz) * scale
            qz = jnp.where(side_lane < lam_lane, qz, 0.0)
            factor = jnp.minimum(wp[rows, :] * lax.rsqrt(qx * qx + qy * qy + qz * qz), 1.0)
            wpx[rows, :] = qx * factor
            wpy[k, rows, :] = qy * factor
            wpz[rows, :] = qz * factor

        side_step(body)
        wpx[first_row:TOP, :] = wpx[first_row:TOP, :] * not_first_x

    def descend_side(k, total=None):
        def body(row):
            rows, before = pl.ds(row, WIDE), pl.ds(row - 1, WIDE)
            qy, qz = wpy[k, rows, :], wpz[rows, :]
            dv = wpx[rows, :] - wpx[before, :] + (qy - pltpu.roll(qy, 1, 1)) + (qz - pltpu.roll(qz, SPAN, 1))
            source, sink = ws[rows, :], wk[rows, :]
            if k:
                w, flow = ww[rows, :], wt[rows, :]
            else:
                w, flow = wl[rows, :] * (1.0 / CC), jnp.minimum(source, sink)
            level = jnp.minimum(source - dv + w, flow + 1.0 / CC)
            after = jnp.maximum(level - sink, 0.0)
            if k < ITERS - 1:
                wt[rows, :] = jnp.minimum(sink, level)
                ww[rows, :] = after
                wj[k, rows, :] = w * STEP - after * (2.0 * STEP)
            else:
                wu[rows, :] = after * CC
                j = side_lane & (SPAN - 1)
                index = row + lax.broadcasted_iota(jnp.int32, (WIDE, LANES), 0)
                inside = (j >= 3) & (j < 6) & (index >= TOP) & (index < end)
                ww[rows, :] = jnp.where(inside, jnp.abs(w - after), 0.0)

        side_step(body)
        if k < ITERS - 1:
            hold_last(wj, k)

    take_in(0)
    take_in(1)
    for z in range(depth):
        for t in range(tiles):
            hold_last(lab, z, t)
    ascend_planes(0, 0, depth)
    take_in(2)
    take_in(3)
    own_copy.wait()
    for copy in lam_halo:
        copy.wait()
    forwards = []
    for n, (_, _, _, _, put) in enumerate(sides):
        copy = remote(own_lam.at[put], low_lam.at[put], fwd_send.at[n], fwd_recv.at[n], (up, x, y))
        copy.start()
        forwards.append(copy)

    def own_window(row):
        rows = pl.ds(row, WIDE)
        for (_, held), strip in zip(arrays, (wl, wp, ws, wk)):
            value = None
            for z in range(depth):
                moved = turned(held[z, edge_tile, rows, :], SPAN * z + 6 - 3 * y)
                value = moved if value is None else jnp.where(side_lane >= SPAN * z, moved, value)
            if strip is wk:
                moved = turned(own_lam[rows, edge_column], lam_lane + 6 - 3 * y)
                value = value + jnp.where(side_lane >= lam_lane, moved * has_above, 0.0)
            strip[rows, :] = value

    side_step(own_window)
    for d in range(wide_rows // (8 * GROUPS)):
        value = None
        for g in range(GROUPS):
            row = first_row + 8 * (d * GROUPS + g)
            moved = turned(own_lam[row : row + 8, edge_column], 8 * g + 6 - 6 * y)
            value = moved if value is None else jnp.where(small >= 8 * g, moved, value)
        packed[8 * d : 8 * d + 8, :] = value
    for n, device in enumerate(((up, x, y), (up, x, y_other))):
        copy = remote(packed, packed_low.at[n], fwd_send.at[2 + n], fwd_recv.at[2 + n], device)
        copy.start()
        forwards.append(copy)

    def pack_window(i, carry):
        off = lane_of(WIDE // 2) & (SPAN - 1)
        value = None
        for g in range(steps):
            rows = pl.ds(pl.multiple_of(first_row + WIDE * g + i * (WIDE // 2), 8), WIDE // 2)
            moves = ((wl, 0, -3), (wp, 3, 0), (ws, 6, 2 + y), (wk, 8, 4 + y))
            for strip, at, shift in moves:
                moved = turned(strip[rows, :], PART * g + shift)
                value = moved if value is None else jnp.where(off >= PART * g + at, moved, value)
        sent[pl.ds(pl.multiple_of(i * (WIDE // 2), 8), WIDE // 2), :] = value
        return carry

    lax.fori_loop(0, 2, pack_window, 0)
    window = remote(sent, other, win_send, win_recv, (r, x, y_other))
    window.start()
    descend_planes(0, 1, depth - 1)
    ascend_planes(1, 1, 2)

    above_bounds = [0] + [CHUNK * c - 3 * HALO for c in range(1, CHUNKS)] + [width_x]
    above_copies = [
        remote(out.at[0, TOP + a : TOP + b], above.at[a:b], up_send.at[c], up_recv.at[c], (down, x, y))
        for c, (a, b) in enumerate(zip(above_bounds[:-1], above_bounds[1:]))
    ]

    for copy in forwards:
        copy.wait()

    def chunk(c, total):
        for n in range(CHUNKS):

            @pl.when(c == n)
            def _():
                lam_copies[n].wait()

        row = pl.multiple_of(first_row + c * CHUNK, 8)
        descend(0, 0, row, CHUNK)
        close_x(0)
        ascend(1, 0, row - 8, CHUNK)
        open_x(0)
        descend(1, 0, row - 8, CHUNK)
        descend(1, 1, row - 8, CHUNK)
        close_x(0)
        close_x(1)
        ascend(2, 0, row - 16, CHUNK)
        open_x(0)
        total = descend(2, 0, row - 16, CHUNK, total, True)
        for n in range(CHUNKS):

            @pl.when(c == n)
            def _():
                above_copies[n].start()

        return total

    total = lax.fori_loop(0, CHUNKS, chunk, jnp.zeros((CHUNK, LANES), jnp.float32))
    err_row = jnp.sum(total, axis=0, keepdims=True)

    window.wait()
    for g in range(steps):
        rows = slice(first_row + WIDE * g, first_row + WIDE * (g + 1))
        off = side_lane & (SPAN - 1)
        theirs = (off >= 6 - 6 * y) & (off < 9 - 6 * y)
        moves = ((wl, 6 - 6 * y), (wp, 3 - 6 * y), (ws, -5 * y), (wk, -2 - 5 * y))
        for strip, shift in moves:
            strip[rows, :] = jnp.where(theirs, turned(other[...], shift - PART * g), strip[rows, :])
    hold_last(wl)
    for n in range(wide_rows // 8):
        d, g = n // GROUPS, n % GROUPS
        rows = slice(first_row + 8 * n, first_row + 8 * n + 8)
        same = turned(packed_low[0, 8 * d : 8 * d + 8, :], 3 * y - 8 * g)
        cross = turned(packed_low[1, 8 * d : 8 * d + 8, :], 6 - 9 * y - 8 * g)
        theirs = (small >= 6 - 6 * y) & (small < 9 - 6 * y)
        lam = jnp.where(theirs, cross, same)
        wk[rows, :] = wk[rows, :] - jnp.where(small < 9, lam * has_below, 0.0)
    for k in range(ITERS):
        ascend_side(k)
        descend_side(k)
    for d in range(wide_rows // (8 * GROUPS)):
        value = None
        for g in range(GROUPS):
            row = first_row + 8 * (d * GROUPS + g)
            moved = pltpu.roll(wu[row : row + 8, :], 8 * g, 1)
            value = moved if value is None else jnp.where(small >= 8 * g, moved, value)
        packed_u[8 * d : 8 * d + 8, :] = value
    down_copy = remote(packed_u, packed_above, fwd_send.at[4], fwd_recv.at[4], (down, x, y))
    down_copy.start()
    err_row = err_row + jnp.sum(ww[first_row : end + HALO, :], axis=0, keepdims=True)

    descend_planes(0, depth - 1, depth)
    ascend_planes(1, 2, depth)
    descend_planes(1, 2, depth)
    ascend_planes(2, 1, depth)

    def last_plane(z, carry):
        def step(i, inner):
            return descend(ITERS - 1, z, pl.multiple_of(TOP + i * BLOCK, 8), BLOCK, inner)

        return lax.fori_loop(0, width_x // BLOCK, step, carry)

    total = lax.fori_loop(1, depth, last_plane, jnp.zeros((BLOCK, LANES), jnp.float32))
    err_row = err_row + jnp.sum(total, axis=0, keepdims=True)

    def edge_of(rows):
        lane = lane_of(rows)
        return (lane >= (1 - y) * (LANES - 3)) & (lane < (1 - y) * (LANES - 3) + 3)

    def patch(z):
        moved = turned(wu[TOP:end, :], 122 - 125 * y - SPAN * z)
        out[z, TOP:end, edge_column] = jnp.where(edge_of(width_x), moved, out[z, TOP:end, edge_column])

    for z in range(1, depth):
        patch(z)
    down_copy.wait()

    gaps = jnp.zeros((8, LANES), jnp.float32)
    edge = edge_of(8)
    for copy, a, b in zip(above_copies, above_bounds[:-1], above_bounds[1:]):
        copy.wait()
        for row in range(a, b, 8):
            n = row // 8 + 1
            d, g = n // GROUPS, n % GROUPS
            moved = turned(packed_above[8 * d : 8 * d + 8, :], 122 - 125 * y - 8 * g)
            above[row : row + 8, edge_column] = jnp.where(edge, moved, above[row : row + 8, edge_column])
        gap = (out[depth - 1, TOP + a : TOP + b, :] - above[a:b, :]) * has_above
        above[a:b, :] = gap
        squares = gap * gap
        for row in range(0, b - a, 8):
            for t in range(tiles):
                gaps = gaps + squares[row : row + 8, t * LANES : (t + 1) * LANES]
    gap_row = jnp.sum(gaps, axis=0, keepdims=True)
    sub = lax.broadcasted_iota(jnp.int32, (8, LANES), 0)
    mine = jnp.where(sub == 0, gap_row, jnp.where(sub == 1, err_row, 0.0))
    n = 0
    for s, stage in enumerate(stages):
        part[s] = mine
        copies = []
        for peer in stage:
            copy = remote(part.at[s, 0:2], got.at[n, 0:2], red_send.at[n], red_recv.at[n], peer)
            copy.start()
            copies.append((copy, n))
            n += 1
        if s == len(stages) - 1:
            patch(0)
        for copy, slot in copies:
            copy.wait()
        for copy, slot in copies:
            mine = mine + got[slot]

    sums = jnp.sum(mine, axis=1, keepdims=True)
    all_cells = depth * width_x * width_y * n_region * n_x * n_y
    plane_cells = (n_region - 1) * width_x * n_x * width_y * n_y
    err = sums[1:2, :] * (CC / all_cells)
    msq = sums[0:1, :] * (1.0 / plane_cells)
    rate = RHO * err * lax.rsqrt(msq + EPSILON)

    def write(i, carry):
        rows = pl.ds(pl.multiple_of(i * BLOCK, 8), BLOCK)
        lam_rows = pl.ds(pl.multiple_of(TOP + i * BLOCK, 8), BLOCK)
        mult[0, rows, :] = own_lam[lam_rows, :] * has_above + above[rows, :] * rate
        return carry

    lax.fori_loop(0, width_x // BLOCK, write, 0)


def write_out(held, held_mult, out, mult, sem):
    depth, width_x, _ = out.shape
    copies = [pltpu.make_async_copy(held.at[z, TOP : TOP + width_x], out.at[z], sem.at[z]) for z in range(depth)]
    copies.append(pltpu.make_async_copy(held_mult, mult, sem.at[depth]))
    for copy in copies:
        copy.start()
    for copy in copies:
        copy.wait()


def on_device(sizes, cap_source, cap_sink, penalty, labels, multiplier):
    depth, width_x, width_y = labels.shape
    tiles = width_y // LANES
    rows = TOP + width_x + BOTTOM
    n_region, n_x, n_y = sizes

    def vmem(*shape):
        return pltpu.VMEM(shape, jnp.float32)

    def dma(*shape):
        return pltpu.SemaphoreType.DMA(shape) if shape else pltpu.SemaphoreType.DMA

    volume = vmem(depth, tiles, rows, LANES)
    plane = vmem(rows, width_y)
    strip = vmem(rows, LANES)
    third = vmem((width_x + 2 * HALO) // 3, LANES)
    peers = 1 + (n_x - 1) + (n_region // 4 - 1) + 3
    compact = (width_x + 2 * HALO) // GROUPS
    held, held_mult = pl.pallas_call(
        functools.partial(kernel, sizes),
        out_shape=[
            pltpu.VMEM((depth, rows, width_y), jnp.float32),
            pltpu.VMEM(multiplier.shape, jnp.float32),
        ],
        in_specs=[pl.BlockSpec(memory_space=pl.ANY)] * 5,
        out_specs=[pl.BlockSpec(memory_space=pltpu.VMEM)] * 2,
        scratch_shapes=[
            volume,
            volume,
            volume,
            volume,
            volume,
            volume,
            volume,
            volume,
            volume,
            plane,
            plane,
            vmem(width_x, width_y),
            vmem(4, 2, depth, HALO, width_y),
            third,
            third,
            strip,
            strip,
            strip,
            strip,
            strip,
            strip,
            strip,
            strip,
            vmem(2, rows, LANES),
            vmem(3, rows, LANES),
            strip,
            vmem(compact, LANES),
            vmem(2, compact, LANES),
            vmem(compact, LANES),
            vmem(compact, LANES),
            vmem(4, 8, LANES),
            vmem(peers, 8, LANES),
            dma(4, tiles),
            dma(),
            dma(5, 2),
            dma(5, 2),
            dma(CHUNKS),
            dma(CHUNKS),
            dma(),
            dma(),
            dma(5),
            dma(5),
            dma(CHUNKS),
            dma(CHUNKS),
            dma(peers),
            dma(peers),
        ],
        compiler_params=pltpu.CompilerParams(collective_id=0, has_side_effects=True, vmem_limit_bytes=52 << 20),
        name="slab_flow",
    )(cap_source, cap_sink, penalty, labels, multiplier)
    return pl.pallas_call(
        write_out,
        out_shape=[
            jax.ShapeDtypeStruct(labels.shape, jnp.float32),
            jax.ShapeDtypeStruct(multiplier.shape, jnp.float32),
        ],
        in_specs=[pl.BlockSpec(memory_space=pl.ANY)] * 2,
        out_specs=[pl.BlockSpec(memory_space=pl.ANY)] * 2,
        scratch_shapes=[dma(depth + 1)],
        compiler_params=pltpu.CompilerParams(vmem_limit_bytes=4 << 20),
        name="write_out",
    )(held, held_mult)


def solution(mesh):
    placed = P("region", "gx", "gy")
    sizes = tuple(mesh.shape[a] for a in ("region", "gx", "gy"))
    return jax.shard_map(
        functools.partial(on_device, sizes),
        mesh=mesh,
        in_specs=(placed,) * 5,
        out_specs=(placed, placed),
        check_vma=False,
    )
```

time: 65.4 us -> 57.6 us (0.88)
  Pallas kernels: 64.7 us -> 56.8 us
    pallas_call x1, Pallas kernels: 62.3 us -> 54.4 us  [on_device(): pl.pallas_call(functools.partial(kernel, sizes), out_shape=[pltpu.VMEM((d...]
where the time goes in v2:
time: 57.6 us; the launch traced here: 57.5 us
  Pallas kernels  56.8 us (99%)
  between operations  0.64 us (1%)
    pallas_call x1, Pallas kernels, on_device(): pl.pallas_call(functools.partial(kernel, sizes), out_shape=[pltpu.VMEM((d...  54.4 us
    pallas_call x1, Pallas kernels, on_device(): pl.pallas_call(write_out, out_shape=[jax.ShapeDtypeStruct(labels.shape, j...  2.4 us

profile of v2, /device:TPU:0, one launch (start us, length us, event | category | flops | bytes accessed | tf_op | source)
XLA Modules:
  0.0 57.5 jit_solution(17379582941971304869)
XLA Ops:
  0.6 54.4 %slab_flow.1 = (f32[4,568,512]{2,1,0:T(8,128)S(1)}, f32[1,512,512]{2,1,0:T(8,128)S(1)}) custom-call(f32[4,512,512]{2,1,0:T(8,128)} %cap_source.1, f32[4,512,512]{2,1,0:T(8,128)} %cap_sink.1, f32[4,512,512]{2,1,0:T(8,128)} %penalty.1, f32[4,512,512]{2,1,0:T(8,128)} %labels.1, f32[1,512,512]{2,1,0:T(8,128)} %multiplier.1), custom_call_target="tpu_custom_call" | custom-call | tf_op jit(solution)/shard_map/slab_flow/pallas_call | solution.py:593
  55.1 2.4 %write_out.1 = (f32[4,512,512]{2,1,0:T(8,128)}, f32[1,512,512]{2,1,0:T(8,128)}) custom-call(f32[4,568,512]{2,1,0:T(8,128)S(1)} %get-tuple-element.4.held, f32[1,512,512]{2,1,0:T(8,128)S(1)} %get-tuple-element.5.held_mult), custom_call_target="tpu_custom_call" | custom-call | tf_op jit(solution)/shard_map/write_out/pallas_call | solution.py:652

commit v3 on v2

--- a/solution.py
+++ b/solution.py
@@ -72,7 +72,8 @@
     packed_u,
     packed_above,
     part,
-    got,
+    got_near,
+    got_far,
     load_sem,
     lam_load_sem,
     halo_send,
@@ -101,20 +102,24 @@
     y_other = 1 - y
     core, high, high_y = lax.rem(r, 2), lax.rem(r // 2, 2), r // 4
     n_rows = n_region // 4
-    stages = (
-        [(4 * high_y + 2 * high + (1 - core), x, y)],
-        [(r, lax.rem(x + d, n_x), y) for d in range(1, n_x)],
-        [(4 * lax.rem(high_y + d, n_rows) + 2 * high + core, x, y) for d in range(1, n_rows)],
-        [
-            (r, x, y_other),
-            (4 * high_y + 2 * (1 - high) + core, x, y),
-            (4 * high_y + 2 * (1 - high) + core, x, y_other),
-        ],
-    )
+    near, far = [], []
+    for dx in range(n_x):
+        for dc in range(2):
+            if dx or dc:
+                at = (4 * high_y + 2 * high + lax.rem(core + dc, 2), lax.rem(x + dx, n_x), y)
+                near.append((min(dx, n_x - dx), at))
+    for dy in range(n_rows):
+        for dh in range(2):
+            for dl in range(2):
+                if dy or dh or dl:
+                    at = (4 * lax.rem(high_y + dy, n_rows) + 2 * lax.rem(high + dh, 2) + core, x, lax.rem(y + dl, 2))
+                    hops = min(dy, n_rows - dy) + (1 if dl else 2 * dh)
+                    far.append((hops, at))
+    stages = [[at for _, at in sorted(stage, key=lambda item: -item[0])] for stage in (near, far)]
 
     barrier = pltpu.get_barrier_semaphore()
     friends = [(up, x, y), (down, x, y), (up, x, y_other), (down, x, y_other)]
-    friends += [peer for stage in stages[1:] for peer in stage]
+    friends += [peer for stage in stages for peer in stage]
     for peer in friends:
         pl.semaphore_signal(barrier, inc=1, device_id=peer, device_id_type=MESH)
 
@@ -132,6 +137,8 @@
             copy.start()
             loads.append(copy)
 
+    own_copy = pltpu.make_async_copy(multiplier.at[0], own_lam.at[TOP:end], lam_load_sem)
+    own_copy.start()
     load(0)
     load(1)
     pl.semaphore_wait(barrier, len(friends))
@@ -141,8 +148,7 @@
         remote(multiplier.at[0, a:b], low_lam.at[TOP + a : TOP + b], lam_send.at[c], lam_recv.at[c], (up, x, y))
         for c, (a, b) in enumerate(zip(lam_bounds[:-1], lam_bounds[1:]))
     ]
-    for copy in lam_copies:
-        copy.start()
+    lam_copies[0].start()
 
     sides = (
         ((r, x_prev, y), slice(0, TAKE), slice(0, TAKE), slice(end, end + HALO), slice(end, end + TAKE)),
@@ -169,19 +175,17 @@
             copy.wait()
         place_halo(q)
 
-    send_halo(0)
-    send_halo(1)
-    load(2)
-    load(3)
-    own_copy = pltpu.make_async_copy(multiplier.at[0], own_lam.at[TOP:end], lam_load_sem)
-    own_copy.start()
-    send_halo(2)
-    send_halo(3)
     lam_halo = []
     for side, (device, take, _, _, put) in enumerate(sides):
         copy = remote(multiplier.at[0, take], own_lam.at[put], halo_send.at[4, side], halo_recv.at[4, side], device)
         copy.start()
         lam_halo.append(copy)
+    send_halo(0)
+    send_halo(1)
+    load(2)
+    load(3)
+    send_halo(2)
+    send_halo(3)
 
     has_above = (r < n_region - 1).astype(jnp.float32)
     has_below = (r > 0).astype(jnp.float32)
@@ -194,6 +198,30 @@
 
     def turned(value, shift):
         return pltpu.roll(value, lax.rem(shift + 4 * LANES, LANES), 1)
+
+    own_copy.wait()
+    for copy in lam_halo:
+        copy.wait()
+    forwards = []
+    for n, (_, _, _, _, put) in enumerate(sides):
+        copy = remote(own_lam.at[put], low_lam.at[put], fwd_send.at[n], fwd_recv.at[n], (up, x, y))
+        copy.start()
+        forwards.append(copy)
+
+    for d in range(wide_rows // (8 * GROUPS)):
+        value = None
+        for g in range(GROUPS):
+            row = first_row + 8 * (d * GROUPS + g)
+            moved = turned(own_lam[row : row + 8, edge_column], 8 * g + 6 - 6 * y)
+            value = moved if value is None else jnp.where(small >= 8 * g, moved, value)
+        packed[8 * d : 8 * d + 8, :] = value
+    for n, device in enumerate(((up, x, y), (up, x, y_other))):
+        copy = remote(packed, packed_low.at[n], fwd_send.at[2 + n], fwd_recv.at[2 + n], device)
+        copy.start()
+        forwards.append(copy)
+
+    for copy in lam_copies[1:]:
+        copy.start()
 
     def hold_last(ref, *at):
         here = ref[(*at, pl.ds(end, 8), slice(None))]
@@ -297,19 +325,15 @@
         planes(low, high, lambda z, row: descend(k, z, row, WIDE), close_x)
 
     def side_step(body):
-        def step(i, carry):
-            body(pl.multiple_of(first_row + i * WIDE, 8))
-            return carry
-
-        lax.fori_loop(0, steps, step, 0)
-
-    side_lane = lane_of(WIDE)
+        body(first_row)
+
+    side_lane = lane_of(wide_rows)
 
     def ascend_side(k):
         field = wj.at[k - 1] if k else wl
 
         def body(row):
-            rows, after = pl.ds(row, WIDE), pl.ds(row + 1, WIDE)
+            rows, after = pl.ds(row, wide_rows), pl.ds(row + 1, wide_rows)
             j = field[rows, :]
             jx = field[after, :]
             jy = pltpu.roll(j, LANES - 1, 1)
@@ -331,7 +355,7 @@
 
     def descend_side(k, total=None):
         def body(row):
-            rows, before = pl.ds(row, WIDE), pl.ds(row - 1, WIDE)
+            rows, before = pl.ds(row, wide_rows), pl.ds(row - 1, wide_rows)
             qy, qz = wpy[k, rows, :], wpz[rows, :]
             dv = wpx[rows, :] - wpx[before, :] + (qy - pltpu.roll(qy, 1, 1)) + (qz - pltpu.roll(qz, SPAN, 1))
             source, sink = ws[rows, :], wk[rows, :]
@@ -348,7 +372,7 @@
             else:
                 wu[rows, :] = after * CC
                 j = side_lane & (SPAN - 1)
-                index = row + lax.broadcasted_iota(jnp.int32, (WIDE, LANES), 0)
+                index = row + lax.broadcasted_iota(jnp.int32, (wide_rows, LANES), 0)
                 inside = (j >= 3) & (j < 6) & (index >= TOP) & (index < end)
                 ww[rows, :] = jnp.where(inside, jnp.abs(w - after), 0.0)
 
@@ -364,40 +388,23 @@
     ascend_planes(0, 0, depth)
     take_in(2)
     take_in(3)
-    own_copy.wait()
-    for copy in lam_halo:
-        copy.wait()
-    forwards = []
-    for n, (_, _, _, _, put) in enumerate(sides):
-        copy = remote(own_lam.at[put], low_lam.at[put], fwd_send.at[n], fwd_recv.at[n], (up, x, y))
-        copy.start()
-        forwards.append(copy)
-
-    def own_window(row):
+    side_lane_part = lane_of(WIDE)
+
+    def own_window(i, carry):
+        row = pl.multiple_of(first_row + i * WIDE, 8)
         rows = pl.ds(row, WIDE)
         for (_, held), strip in zip(arrays, (wl, wp, ws, wk)):
             value = None
             for z in range(depth):
                 moved = turned(held[z, edge_tile, rows, :], SPAN * z + 6 - 3 * y)
-                value = moved if value is None else jnp.where(side_lane >= SPAN * z, moved, value)
+                value = moved if value is None else jnp.where(side_lane_part >= SPAN * z, moved, value)
             if strip is wk:
                 moved = turned(own_lam[rows, edge_column], lam_lane + 6 - 3 * y)
-                value = value + jnp.where(side_lane >= lam_lane, moved * has_above, 0.0)
+                value = value + jnp.where(side_lane_part >= lam_lane, moved * has_above, 0.0)
             strip[rows, :] = value
-
-    side_step(own_window)
-    for d in range(wide_rows // (8 * GROUPS)):
-        value = None
-        for g in range(GROUPS):
-            row = first_row + 8 * (d * GROUPS + g)
-            moved = turned(own_lam[row : row + 8, edge_column], 8 * g + 6 - 6 * y)
-            value = moved if value is None else jnp.where(small >= 8 * g, moved, value)
-        packed[8 * d : 8 * d + 8, :] = value
-    for n, device in enumerate(((up, x, y), (up, x, y_other))):
-        copy = remote(packed, packed_low.at[n], fwd_send.at[2 + n], fwd_recv.at[2 + n], device)
-        copy.start()
-        forwards.append(copy)
-
+        return carry
+
+    lax.fori_loop(0, steps, own_window, 0)
     def pack_window(i, carry):
         off = lane_of(WIDE // 2) & (SPAN - 1)
         value = None
@@ -422,7 +429,7 @@
         for c, (a, b) in enumerate(zip(above_bounds[:-1], above_bounds[1:]))
     ]
 
-    for copy in forwards:
+    for copy in forwards[:2]:
         copy.wait()
 
     def chunk(c, total):
@@ -456,9 +463,11 @@
     err_row = jnp.sum(total, axis=0, keepdims=True)
 
     window.wait()
+    for copy in forwards[2:]:
+        copy.wait()
     for g in range(steps):
         rows = slice(first_row + WIDE * g, first_row + WIDE * (g + 1))
-        off = side_lane & (SPAN - 1)
+        off = side_lane_part & (SPAN - 1)
         theirs = (off >= 6 - 6 * y) & (off < 9 - 6 * y)
         moves = ((wl, 6 - 6 * y), (wp, 3 - 6 * y), (ws, -5 * y), (wk, -2 - 5 * y))
         for strip, shift in moves:
@@ -530,21 +539,19 @@
     gap_row = jnp.sum(gaps, axis=0, keepdims=True)
     sub = lax.broadcasted_iota(jnp.int32, (8, LANES), 0)
     mine = jnp.where(sub == 0, gap_row, jnp.where(sub == 1, err_row, 0.0))
-    n = 0
-    for s, stage in enumerate(stages):
+    sends = []
+    for s, (stage, got) in enumerate(zip(stages, (got_near, got_far))):
         part[s] = mine
-        copies = []
-        for peer in stage:
-            copy = remote(part.at[s, 0:2], got.at[n, 0:2], red_send.at[n], red_recv.at[n], peer)
+        for n, peer in enumerate(stage):
+            copy = remote(part.at[s, 0:2], got.at[n, 0:2], red_send.at[s, n], red_recv.at[s], peer)
             copy.start()
-            copies.append((copy, n))
-            n += 1
+            sends.append(copy)
         if s == len(stages) - 1:
             patch(0)
-        for copy, slot in copies:
-            copy.wait()
-        for copy, slot in copies:
-            mine = mine + got[slot]
+        pltpu.make_async_copy(got.at[:, 0:2], got.at[:, 0:2], red_recv.at[s]).wait()
+        mine = mine + jnp.sum(got[...], axis=0)
+    for copy in sends:
+        copy.wait_send()
 
     sums = jnp.sum(mine, axis=1, keepdims=True)
     all_cells = depth * width_x * width_y * n_region * n_x * n_y
@@ -588,7 +595,7 @@
     plane = vmem(rows, width_y)
     strip = vmem(rows, LANES)
     third = vmem((width_x + 2 * HALO) // 3, LANES)
-    peers = 1 + (n_x - 1) + (n_region // 4 - 1) + 3
+    near, far = 2 * n_x - 1, n_region - 1
     compact = (width_x + 2 * HALO) // GROUPS
     held, held_mult = pl.pallas_call(
         functools.partial(kernel, sizes),
@@ -629,8 +636,9 @@
             vmem(2, compact, LANES),
             vmem(compact, LANES),
             vmem(compact, LANES),
-            vmem(4, 8, LANES),
-            vmem(peers, 8, LANES),
+            vmem(2, 8, LANES),
+            vmem(near, 8, LANES),
+            vmem(far, 8, LANES),
             dma(4, tiles),
             dma(),
             dma(5, 2),
@@ -643,8 +651,8 @@
             dma(5),
             dma(CHUNKS),
             dma(CHUNKS),
-            dma(peers),
-            dma(peers),
+            dma(2, far),
+            dma(2),
         ],
         compiler_params=pltpu.CompilerParams(collective_id=0, has_side_effects=True, vmem_limit_bytes=52 << 20),
         name="slab_flow",

time: 57.6 us -> 50.7 us (0.88)
  Pallas kernels: 56.8 us -> 49.7 us
    pallas_call x1, Pallas kernels: 54.4 us -> 47.3 us  [on_device(): pl.pallas_call(functools.partial(kernel, sizes), out_shape=[pltpu.VMEM((d...]
where the time goes in v3:
time: 50.7 us; the launch traced here: 50.3 us
  Pallas kernels  49.7 us (98%)
  between operations  0.64 us (1%)
    pallas_call x1, Pallas kernels, on_device(): pl.pallas_call(functools.partial(kernel, sizes), out_shape=[pltpu.VMEM((d...  47.3 us
    pallas_call x1, Pallas kernels, on_device(): pl.pallas_call(write_out, out_shape=[jax.ShapeDtypeStruct(labels.shape, j...  2.4 us

profile of v3, /device:TPU:0, one launch (start us, length us, event | category | flops | bytes accessed | tf_op | source)
XLA Modules:
  0.0 50.3 jit_solution(390901176331719988)
XLA Ops:
  0.6 47.3 %slab_flow.1 = (f32[4,568,512]{2,1,0:T(8,128)S(1)}, f32[1,512,512]{2,1,0:T(8,128)S(1)}) custom-call(f32[4,512,512]{2,1,0:T(8,128)} %cap_source.1, f32[4,512,512]{2,1,0:T(8,128)} %cap_sink.1, f32[4,512,512]{2,1,0:T(8,128)} %penalty.1, f32[4,512,512]{2,1,0:T(8,128)} %labels.1, f32[1,512,512]{2,1,0:T(8,128)} %multiplier.1), custom_call_target="tpu_custom_call" | custom-call | tf_op jit(solution)/shard_map/slab_flow/pallas_call | solution.py:600
  47.9 2.4 %write_out.1 = (f32[4,512,512]{2,1,0:T(8,128)}, f32[1,512,512]{2,1,0:T(8,128)}) custom-call(f32[4,568,512]{2,1,0:T(8,128)S(1)} %get-tuple-element.4.held, f32[1,512,512]{2,1,0:T(8,128)S(1)} %get-tuple-element.5.held_mult), custom_call_target="tpu_custom_call" | custom-call | tf_op jit(solution)/shard_map/write_out/pallas_call | solution.py:660

commit v4 on v3

--- a/solution.py
+++ b/solution.py
@@ -16,16 +16,17 @@
 
 LANES = 128
 TOP = 32
-BOTTOM = 24
+BOTTOM = 32
 HALO = 8
 TAKE = 4
 SPAN = 32
 PART = 10
 GROUPS = 11
 WIDE = 176
-BLOCK = 128
-CHUNKS = 4
-CHUNK = 136
+BLOCK = 256
+CHUNKS = 3
+CHUNK = 184
+EARLY = 9
 
 
 def lane_of(rows):
@@ -120,8 +121,11 @@
     barrier = pltpu.get_barrier_semaphore()
     friends = [(up, x, y), (down, x, y), (up, x, y_other), (down, x, y_other)]
     friends += [peer for stage in stages for peer in stage]
-    for peer in friends:
-        pl.semaphore_signal(barrier, inc=1, device_id=peer, device_id_type=MESH)
+    friends.sort(key=lambda peer: peer[1] is x)
+
+    def greet(peers):
+        for peer in peers:
+            pl.semaphore_signal(barrier, inc=1, device_id=peer, device_id_type=MESH)
 
     def remote(a, b, s, t, device):
         return pltpu.make_async_remote_copy(a, b, s, t, device_id=device, device_id_type=MESH)
@@ -138,9 +142,11 @@
             loads.append(copy)
 
     own_copy = pltpu.make_async_copy(multiplier.at[0], own_lam.at[TOP:end], lam_load_sem)
+    greet(friends[:EARLY])
     own_copy.start()
     load(0)
     load(1)
+    greet(friends[EARLY:])
     pl.semaphore_wait(barrier, len(friends))
 
     lam_bounds = [0] + [CHUNK * c - HALO for c in range(1, CHUNKS)] + [width_x]
@@ -390,21 +396,19 @@
     take_in(3)
     side_lane_part = lane_of(WIDE)
 
-    def own_window(i, carry):
-        row = pl.multiple_of(first_row + i * WIDE, 8)
-        rows = pl.ds(row, WIDE)
+    def own_window(row):
+        rows = pl.ds(row, wide_rows)
         for (_, held), strip in zip(arrays, (wl, wp, ws, wk)):
             value = None
             for z in range(depth):
                 moved = turned(held[z, edge_tile, rows, :], SPAN * z + 6 - 3 * y)
-                value = moved if value is None else jnp.where(side_lane_part >= SPAN * z, moved, value)
+                value = moved if value is None else jnp.where(side_lane >= SPAN * z, moved, value)
             if strip is wk:
                 moved = turned(own_lam[rows, edge_column], lam_lane + 6 - 3 * y)
-                value = value + jnp.where(side_lane_part >= lam_lane, moved * has_above, 0.0)
+                value = value + jnp.where(side_lane >= lam_lane, moved * has_above, 0.0)
             strip[rows, :] = value
-        return carry
-
-    lax.fori_loop(0, steps, own_window, 0)
+
+    side_step(own_window)
     def pack_window(i, carry):
         off = lane_of(WIDE // 2) & (SPAN - 1)
         value = None
@@ -433,6 +437,11 @@
         copy.wait()
 
     def chunk(c, total):
+        @pl.when(c == CHUNKS - 1)
+        def _():
+            descend_planes(0, depth - 1, depth)
+            ascend_planes(1, 2, depth)
+
         for n in range(CHUNKS):
 
             @pl.when(c == n)
@@ -495,8 +504,6 @@
     down_copy.start()
     err_row = err_row + jnp.sum(ww[first_row : end + HALO, :], axis=0, keepdims=True)
 
-    descend_planes(0, depth - 1, depth)
-    ascend_planes(1, 2, depth)
     descend_planes(1, 2, depth)
     ascend_planes(2, 1, depth)
 
@@ -521,7 +528,7 @@
         patch(z)
     down_copy.wait()
 
-    gaps = jnp.zeros((8, LANES), jnp.float32)
+    gaps = [jnp.zeros((8, LANES), jnp.float32)] * (2 * tiles)
     edge = edge_of(8)
     for copy, a, b in zip(above_copies, above_bounds[:-1], above_bounds[1:]):
         copy.wait()
@@ -535,8 +542,9 @@
         squares = gap * gap
         for row in range(0, b - a, 8):
             for t in range(tiles):
-                gaps = gaps + squares[row : row + 8, t * LANES : (t + 1) * LANES]
-    gap_row = jnp.sum(gaps, axis=0, keepdims=True)
+                n = 2 * t + row // 8 % 2
+                gaps[n] = gaps[n] + squares[row : row + 8, t * LANES : (t + 1) * LANES]
+    gap_row = jnp.sum(sum(gaps[1:], gaps[0]), axis=0, keepdims=True)
     sub = lax.broadcasted_iota(jnp.int32, (8, LANES), 0)
     mine = jnp.where(sub == 0, gap_row, jnp.where(sub == 1, err_row, 0.0))
     sends = []
@@ -560,13 +568,7 @@
     msq = sums[0:1, :] * (1.0 / plane_cells)
     rate = RHO * err * lax.rsqrt(msq + EPSILON)
 
-    def write(i, carry):
-        rows = pl.ds(pl.multiple_of(i * BLOCK, 8), BLOCK)
-        lam_rows = pl.ds(pl.multiple_of(TOP + i * BLOCK, 8), BLOCK)
-        mult[0, rows, :] = own_lam[lam_rows, :] * has_above + above[rows, :] * rate
-        return carry
-
-    lax.fori_loop(0, width_x // BLOCK, write, 0)
+    mult[0] = own_lam[TOP:end, :] * has_above + above[...] * rate
 
 
 def write_out(held, held_mult, out, mult, sem):

time: 50.7 us -> 49.9 us (0.984)
  Pallas kernels: 49.7 us -> 48.9 us
    pallas_call x1, Pallas kernels: 47.3 us -> 46.6 us  [on_device(): pl.pallas_call(functools.partial(kernel, sizes), out_shape=[pltpu.VMEM((d...]
where the time goes in v4:
time: 49.9 us; the launch traced here: 49.6 us
  Pallas kernels  48.9 us (98%)
  between operations  0.64 us (1%)
    pallas_call x1, Pallas kernels, on_device(): pl.pallas_call(functools.partial(kernel, sizes), out_shape=[pltpu.VMEM((d...  46.6 us
    pallas_call x1, Pallas kernels, on_device(): pl.pallas_call(write_out, out_shape=[jax.ShapeDtypeStruct(labels.shape, j...  2.4 us

profile of v4, /device:TPU:0, one launch (start us, length us, event | category | flops | bytes accessed | tf_op | source)
XLA Modules:
  0.0 49.6 jit_solution(13584582088358417681)
XLA Ops:
  0.6 46.6 %slab_flow.1 = (f32[4,576,512]{2,1,0:T(8,128)S(1)}, f32[1,512,512]{2,1,0:T(8,128)S(1)}) custom-call(f32[4,512,512]{2,1,0:T(8,128)} %cap_source.1, f32[4,512,512]{2,1,0:T(8,128)} %cap_sink.1, f32[4,512,512]{2,1,0:T(8,128)} %penalty.1, f32[4,512,512]{2,1,0:T(8,128)} %labels.1, f32[1,512,512]{2,1,0:T(8,128)} %multiplier.1), custom_call_target="tpu_custom_call" | custom-call | tf_op jit(solution)/shard_map/slab_flow/pallas_call | solution.py:602
  47.2 2.4 %write_out.1 = (f32[4,512,512]{2,1,0:T(8,128)}, f32[1,512,512]{2,1,0:T(8,128)}) custom-call(f32[4,576,512]{2,1,0:T(8,128)S(1)} %get-tuple-element.4.held, f32[1,512,512]{2,1,0:T(8,128)S(1)} %get-tuple-element.5.held_mult), custom_call_target="tpu_custom_call" | custom-call | tf_op jit(solution)/shard_map/write_out/pallas_call | solution.py:662

commit v5 on v4

--- a/solution.py
+++ b/solution.py
@@ -23,7 +23,7 @@
 PART = 10
 GROUPS = 11
 WIDE = 176
-BLOCK = 256
+BLOCK = 128
 CHUNKS = 3
 CHUNK = 184
 EARLY = 9
@@ -505,11 +505,47 @@
     err_row = err_row + jnp.sum(ww[first_row : end + HALO, :], axis=0, keepdims=True)
 
     descend_planes(1, 2, depth)
-    ascend_planes(2, 1, depth)
+
+    def finish(z, row, count, total):
+        rows, after, before = pl.ds(row, count), pl.ds(row + 1, count), pl.ds(row - 1, count)
+        lane = lane_of(count)
+        here = [jj[z, t, rows, :] for t in range(tiles)]
+        rolled = [pltpu.roll(v, LANES - 1, 1) for v in here]
+        flows = []
+        for t in range(tiles):
+            j = here[t]
+            jy = jnp.where(lane == LANES - 1, rolled[t + 1] if t < tiles - 1 else j, rolled[t])
+            qx = px[z, t, rows, :] + (jj[z, t, after, :] - j)
+            qy = py[z, t, rows, :] + (jy - j)
+            qz = pz[z, t, rows, :] + (jj[jnp.minimum(z + 1, depth - 1), t, rows, :] - j)
+            factor = jnp.minimum(pen[z, t, rows, :] * lax.rsqrt(qx * qx + qy * qy + qz * qz), 1.0)
+            qx, qy, qz = qx * factor, qy * factor, qz * factor
+            px[z, t, rows, :] = qx
+            pz[z, t, rows, :] = qz
+            flows.append((qx, qy, qz))
+        turned_y = [pltpu.roll(flow[1], 1, 1) for flow in flows]
+        for t in range(tiles):
+            qx, qy, qz = flows[t]
+            dv = qx - px[z, t, before, :] + (qy - jnp.where(lane == 0, turned_y[t - 1] if t else 0.0, turned_y[t]))
+            dv = dv + qz - pz[z - 1, t, rows, :]
+            sink, w = snk[z, t, rows, :], lab[z, t, rows, :]
+            level = jnp.minimum(src[z, t, rows, :] - dv + w, pt[z, t, rows, :] + 1.0 / CC)
+            new = jnp.maximum(level - sink, 0.0)
+            out[z, rows, t * LANES : (t + 1) * LANES] = new * CC
+            change = jnp.abs(w - new)
+            if t == 0:
+                change = jnp.where((lane < 3) & (y == 1), 0.0, change)
+            if t == tiles - 1:
+                change = jnp.where((lane >= LANES - 3) & (y == 0), 0.0, change)
+            total = total + change
+        return total
 
     def last_plane(z, carry):
+        ascend(2, z, first_row, HALO)
+        open_x(z)
+
         def step(i, inner):
-            return descend(ITERS - 1, z, pl.multiple_of(TOP + i * BLOCK, 8), BLOCK, inner)
+            return finish(z, pl.multiple_of(TOP + i * BLOCK, 8), BLOCK, inner)
 
         return lax.fori_loop(0, width_x // BLOCK, step, carry)
 

time: 49.9 us -> 49.9 us (level)
  no operation moved by 1% of the time
where the time goes in v5:
time: 49.9 us; the launch traced here: 49.6 us
  Pallas kernels  49 us (98%)
  between operations  0.64 us (1%)
    pallas_call x1, Pallas kernels, on_device(): pl.pallas_call(functools.partial(kernel, sizes), out_shape=[pltpu.VMEM((d...  46.6 us
    pallas_call x1, Pallas kernels, on_device(): pl.pallas_call(write_out, out_shape=[jax.ShapeDtypeStruct(labels.shape, j...  2.4 us

profile of v5, /device:TPU:0, one launch (start us, length us, event | category | flops | bytes accessed | tf_op | source)
XLA Modules:
  0.0 49.6 jit_solution(8300952904755454580)
XLA Ops:
  0.6 46.6 %slab_flow.1 = (f32[4,576,512]{2,1,0:T(8,128)S(1)}, f32[1,512,512]{2,1,0:T(8,128)S(1)}) custom-call(f32[4,512,512]{2,1,0:T(8,128)} %cap_source.1, f32[4,512,512]{2,1,0:T(8,128)} %cap_sink.1, f32[4,512,512]{2,1,0:T(8,128)} %penalty.1, f32[4,512,512]{2,1,0:T(8,128)} %labels.1, f32[1,512,512]{2,1,0:T(8,128)} %multiplier.1), custom_call_target="tpu_custom_call" | custom-call | tf_op jit(solution)/shard_map/slab_flow/pallas_call | solution.py:638
  47.2 2.4 %write_out.1 = (f32[4,512,512]{2,1,0:T(8,128)}, f32[1,512,512]{2,1,0:T(8,128)}) custom-call(f32[4,576,512]{2,1,0:T(8,128)S(1)} %get-tuple-element.4.held, f32[1,512,512]{2,1,0:T(8,128)S(1)} %get-tuple-element.5.held_mult), custom_call_target="tpu_custom_call" | custom-call | tf_op jit(solution)/shard_map/write_out/pallas_call | solution.py:698
